TPU v7x, 32 devices: a whole 2x2x4 slice. The times are simulated.
32 devices in a mesh: fsdp: 8 (over z, y), seq: 4 (over x, core).
Axes of the slice: x: 2, y: 2, z: 4, core: 2. Of those that a mesh axis runs over, the one named last changes fastest.
Arguments:
- inputs: bfloat16 [3, 8, 1024, 768], P(None, 'fsdp', 'seq'), may hold values from -6 to 6
- segments: int32 [3, 8, 1024], P(None, 'fsdp'), may hold values from 0 to 5, never falling along the last dimension, each value on 1 to 512 neighbouring positions
- cotangent: bfloat16 [3, 8, 1024, 768], P(None, 'fsdp', 'seq'), may hold values from -6 to 6
- w_qkv: bfloat16 [768, 2304], P('fsdp'), may hold values from -0.21875 to 0.21875
- w_out: bfloat16 [768, 768], P('fsdp'), may hold values from -1.75 to 1.75
- w_up: bfloat16 [768, 3072], P('fsdp'), may hold values from -0.21875 to 0.21875
- w_down: bfloat16 [3072, 768], P('fsdp'), may hold values from -0.15625 to 0.15625
- vectors: bfloat16 [768, 8], P('fsdp'), may hold values from -1 to 1.5
- bias_up: bfloat16 [3072], P('fsdp'), may hold values from -1.5 to 1.5
Outputs:
- result: bfloat16 [3, 8, 1024, 768], P(None, 'fsdp', 'seq')
- grad_input: float32 [3, 8, 1024, 768], P(None, 'fsdp', 'seq')
- grad_qkv: float32 [768, 2304], P('fsdp')
- grad_outproj: float32 [768, 768], P('fsdp')
- grad_up: float32 [768, 3072], P('fsdp')
- grad_down: float32 [3072, 768], P('fsdp')
- grad_vectors: float32 [768, 8], P('fsdp')
- grad_bias_up: float32 [3072], P('fsdp')
Inputs may be any that keep to these rules, and one draw needn't show every extreme that they name: `segments`: along each sequence the segment numbers never fall; every one of the 6 numbers holds 1 to 512 tokens of a sequence, and the longest holds exactly 512.
All inputs are finite; a program needn't handle non-finite values.
Results may differ from a plain program's by a relative error of at most 0.014.
Values may be sent and summed in bfloat16 or wider, within the bound.
No kernel may reach another device: no remote copies, remote signals or barrier semaphores. Data moves between devices by JAX's collectives and lax.ppermute only.
A program may use at most 320 MiB of HBM per device.

v0:
```python
import jax
import jax.numpy as jnp
from jax import lax
from jax.sharding import PartitionSpec as P

HEADS = 12
HEAD_DIM = 64


epsilon = 1e-05
masked_value = -1e30


def smooth_gate(values):
    return jax.nn.gelu(values, approximate=True)


def norm_parts(values, gain, shift):
    average = jnp.mean(values, axis=-1, keepdims=True)
    centred = values - average
    spread = jnp.mean(centred * centred, axis=-1, keepdims=True)
    inverse = lax.rsqrt(spread + epsilon)
    normal = centred * inverse
    return (normal * gain + shift, normal, inverse)


def norm_back(grad_normed, normal, inverse, gain):
    scaled = grad_normed * gain
    first = jnp.mean(scaled, axis=-1, keepdims=True)
    second = jnp.mean(scaled * normal, axis=-1, keepdims=True)
    return inverse * (scaled - first - normal * second)


def row_block(tensor, row_index, offset, block_rows, axis_pos):
    picked = lax.dynamic_index_in_dim(tensor, row_index, 0, keepdims=False)
    return lax.dynamic_slice_in_dim(picked, offset, block_rows, axis_pos)


def row_whole(tensor, row_index):
    return lax.dynamic_index_in_dim(tensor, row_index, 0, keepdims=False)


def masked_scores(queries, keys_part, segment_rows, row_index, offset, block_rows):
    query_block = row_block(queries, row_index, offset, block_rows, 1)
    keys_row = row_whole(keys_part, row_index)
    segment_row = row_whole(segment_rows, row_index)
    segment_block = lax.dynamic_slice_in_dim(segment_row, offset, block_rows, 0)
    scores = jnp.einsum("hqe,hke->hqk", query_block, keys_row, preferred_element_type=jnp.float32)
    inside = segment_block[:, None] == segment_row[None, :]
    return (jnp.where(inside[None], scores, masked_value), query_block, keys_row)


def attend_forward(queries, keys_part, values_part, segment_rows):
    row_count, heads_local, length, head_size = queries.shape
    block_rows = min(512, length)
    per_row = length // block_rows

    def one_block(position):
        row_index = position // per_row
        offset = position % per_row * block_rows
        scores, query_block, keys_row = masked_scores(
            queries, keys_part, segment_rows, row_index, offset, block_rows
        )
        row_max = jnp.max(scores, axis=-1, keepdims=True)
        raised = jnp.exp(scores - row_max)
        denominator = jnp.sum(raised, axis=-1, keepdims=True)
        probability = (raised / denominator).astype(jnp.bfloat16)
        values_row = row_whole(values_part, row_index)
        context = jnp.einsum(
            "hqk,hke->hqe", probability, values_row, preferred_element_type=jnp.float32
        )
        return (context.astype(jnp.bfloat16), (row_max + jnp.log(denominator))[..., 0])

    contexts, log_sums = lax.map(one_block, jnp.arange(row_count * per_row))
    contexts = contexts.reshape(row_count, per_row, heads_local, block_rows, head_size)
    contexts = contexts.transpose(0, 2, 1, 3, 4).reshape(row_count, heads_local, length, head_size)
    log_sums = log_sums.reshape(row_count, per_row, heads_local, block_rows)
    log_sums = log_sums.transpose(0, 2, 1, 3).reshape(row_count, heads_local, length)
    return (contexts, log_sums)


def attend_backward(queries, keys_part, values_part, segment_rows, log_sums, grad_context):
    row_count, heads_local, length, head_size = queries.shape
    block_rows = min(512, length)
    per_row = length // block_rows

    def one_block(carried, position):
        grad_keys, grad_values = carried
        row_index = position // per_row
        offset = position % per_row * block_rows
        scores, query_block, keys_row = masked_scores(
            queries, keys_part, segment_rows, row_index, offset, block_rows
        )
        lse_block = row_block(log_sums, row_index, offset, block_rows, 1)
        probability = jnp.exp(scores - lse_block[..., None])
        grad_block = row_block(grad_context, row_index, offset, block_rows, 1)
        values_row = row_whole(values_part, row_index)
        grad_prob = jnp.einsum(
            "hqe,hke->hqk", grad_block, values_row, preferred_element_type=jnp.float32
        )
        delta_sum = jnp.sum(grad_prob * probability, axis=-1, keepdims=True)
        grad_scores = (probability * (grad_prob - delta_sum)).astype(jnp.bfloat16)
        grad_query = jnp.einsum(
            "hqk,hke->hqe", grad_scores, keys_row, preferred_element_type=jnp.float32
        )
        key_term = jnp.einsum(
            "hqk,hqe->hke", grad_scores, query_block, preferred_element_type=jnp.float32
        )
        value_term = jnp.einsum(
            "hqk,hqe->hke",
            probability.astype(jnp.bfloat16),
            grad_block,
            preferred_element_type=jnp.float32,
        )
        grad_keys = grad_keys.at[row_index].add(key_term)
        grad_values = grad_values.at[row_index].add(value_term)
        return ((grad_keys, grad_values), grad_query.astype(jnp.bfloat16))

    starting = (jnp.zeros(queries.shape, jnp.float32), jnp.zeros(queries.shape, jnp.float32))
    (grad_keys, grad_values), grad_queries = lax.scan(
        one_block, starting, jnp.arange(row_count * per_row)
    )
    grad_queries = grad_queries.reshape(row_count, per_row, heads_local, block_rows, head_size)
    grad_queries = grad_queries.transpose(0, 2, 1, 3, 4).reshape(
        row_count, heads_local, length, head_size
    )
    return (grad_queries, grad_keys.astype(jnp.bfloat16), grad_values.astype(jnp.bfloat16))


def share_gradients(terms):
    shares = (
        lax.psum_scatter(terms[0], "fsdp", scatter_dimension=0, tiled=True),
        lax.psum_scatter(terms[1], "fsdp", scatter_dimension=0, tiled=True),
        lax.psum_scatter(terms[2], "fsdp", scatter_dimension=0, tiled=True),
        lax.psum_scatter(terms[3], "fsdp", scatter_dimension=0, tiled=True),
        lax.psum_scatter(terms[4], "fsdp", scatter_dimension=0, tiled=True),
        lax.psum_scatter(terms[5], "fsdp", scatter_dimension=0, tiled=True),
    )
    return (
        lax.psum(shares[0].astype(jnp.bfloat16), "seq").astype(jnp.float32),
        lax.psum(shares[1].astype(jnp.bfloat16), "seq").astype(jnp.float32),
        lax.psum(shares[2].astype(jnp.bfloat16), "seq").astype(jnp.float32),
        lax.psum(shares[3].astype(jnp.bfloat16), "seq").astype(jnp.float32),
        lax.psum(shares[4].astype(jnp.bfloat16), "seq").astype(jnp.float32),
        lax.psum(shares[5].astype(jnp.bfloat16), "seq").astype(jnp.float32),
    )


def shards(inputs, segments, cotangent, w_qkv, w_out, w_up, w_down, vectors, bias_up):
    micro_count, row_count, tokens_local, width = inputs.shape
    groups_seq = lax.axis_size("seq")
    heads_local = HEADS // groups_seq
    flat_rows = row_count * tokens_local
    length = tokens_local * groups_seq
    outputs = []
    input_grads = []
    totals = None
    for micro in range(micro_count):
        gathered = (
            lax.all_gather(w_qkv, "fsdp", axis=0, tiled=True),
            lax.all_gather(w_out, "fsdp", axis=0, tiled=True),
            lax.all_gather(w_up, "fsdp", axis=0, tiled=True),
            lax.all_gather(w_down, "fsdp", axis=0, tiled=True),
            lax.all_gather(vectors, "fsdp", axis=0, tiled=True),
            lax.all_gather(bias_up, "fsdp", axis=0, tiled=True),
        )
        qkv_full, out_full, up_full, down_full, vector_full, bias_full = gathered
        vector_f32 = vector_full.astype(jnp.float32)
        flat_in = inputs[micro].astype(jnp.float32).reshape(flat_rows, width)
        normed_a, unit_a, inverse_a = norm_parts(flat_in, vector_f32[:, 0], vector_f32[:, 1])
        normed_a = normed_a.astype(jnp.bfloat16)
        project = jnp.dot(normed_a, qkv_full, preferred_element_type=jnp.float32)
        queries = ((project[:, :width] + vector_f32[:, 2]) * 0.125).astype(jnp.bfloat16)
        keys_part = project[:, width : 2 * width].astype(jnp.bfloat16)
        values_part = (project[:, 2 * width :] + vector_f32[:, 3]).astype(jnp.bfloat16)
        stacked = jnp.stack([queries, keys_part, values_part]).reshape(
            3, row_count, tokens_local, width
        )
        by_heads = lax.all_to_all(stacked, "seq", split_axis=3, concat_axis=2, tiled=True)
        by_heads = by_heads.reshape(3, row_count, length, heads_local, HEAD_DIM).transpose(
            0, 1, 3, 2, 4
        )
        segment_rows = segments[micro]
        contexts, log_sums = attend_forward(by_heads[0], by_heads[1], by_heads[2], segment_rows)
        context_send = contexts.transpose(0, 2, 1, 3).reshape(
            row_count, length, heads_local * HEAD_DIM
        )
        context_tok = lax.all_to_all(
            context_send, "seq", split_axis=1, concat_axis=2, tiled=True
        ).reshape(flat_rows, width)
        attended = (
            jnp.dot(context_tok, out_full, preferred_element_type=jnp.float32) + vector_f32[:, 4]
        )
        middle = flat_in + attended
        normed_b, unit_b, inverse_b = norm_parts(middle, vector_f32[:, 5], vector_f32[:, 6])
        normed_b = normed_b.astype(jnp.bfloat16)
        hidden = jnp.dot(normed_b, up_full, preferred_element_type=jnp.float32) + bias_full.astype(
            jnp.float32
        )
        gated, gate_pullback = jax.vjp(smooth_gate, hidden)
        active = gated.astype(jnp.bfloat16)
        branch = jnp.dot(active, down_full, preferred_element_type=jnp.float32) + vector_f32[:, 7]
        outputs.append(
            (middle + branch).astype(jnp.bfloat16).reshape(row_count, tokens_local, width)
        )
        back_full = (
            lax.all_gather(w_qkv, "fsdp", axis=0, tiled=True),
            lax.all_gather(w_out, "fsdp", axis=0, tiled=True),
            lax.all_gather(w_up, "fsdp", axis=0, tiled=True),
            lax.all_gather(w_down, "fsdp", axis=0, tiled=True),
            lax.all_gather(vectors, "fsdp", axis=0, tiled=True),
        )
        qkv_back, out_back, up_back, down_back, vector_back = back_full
        gain_a = vector_back[:, 0].astype(jnp.float32)
        gain_b = vector_back[:, 5].astype(jnp.float32)
        grad_branch = cotangent[micro].reshape(flat_rows, width)
        grad_result = grad_branch.astype(jnp.float32)
        grad_down = jnp.einsum("tf,td->fd", active, grad_branch, preferred_element_type=jnp.float32)
        bias_down_grad = jnp.sum(grad_result, axis=0)
        grad_active = jnp.einsum(
            "td,fd->tf", grad_branch, down_back, preferred_element_type=jnp.float32
        )
        grad_hidden = gate_pullback(grad_active)[0].astype(jnp.bfloat16)
        grad_up = jnp.einsum("td,tf->df", normed_b, grad_hidden, preferred_element_type=jnp.float32)
        bias_up_grad = jnp.sum(grad_hidden.astype(jnp.float32), axis=0)
        grad_normed_b = jnp.einsum(
            "tf,df->td", grad_hidden, up_back, preferred_element_type=jnp.float32
        )
        gain_b_grad = jnp.sum(grad_normed_b * unit_b, axis=0)
        shift_b_grad = jnp.sum(grad_normed_b, axis=0)
        grad_middle = grad_result + norm_back(grad_normed_b, unit_b, inverse_b, gain_b)
        grad_attended = grad_middle.astype(jnp.bfloat16)
        grad_outproj = jnp.einsum(
            "te,td->ed", context_tok, grad_attended, preferred_element_type=jnp.float32
        )
        bias_out_grad = jnp.sum(grad_attended.astype(jnp.float32), axis=0)
        grad_context = jnp.einsum(
            "td,ed->te", grad_attended, out_back, preferred_element_type=jnp.float32
        ).astype(jnp.bfloat16)
        grad_heads = lax.all_to_all(
            grad_context.reshape(row_count, tokens_local, width),
            "seq",
            split_axis=2,
            concat_axis=1,
            tiled=True,
        )
        grad_heads = grad_heads.reshape(row_count, length, heads_local, HEAD_DIM).transpose(
            0, 2, 1, 3
        )
        grad_q, grad_k, grad_v = attend_backward(
            by_heads[0], by_heads[1], by_heads[2], segment_rows, log_sums, grad_heads
        )
        stacked_grads = jnp.stack([grad_q, grad_k, grad_v]).transpose(0, 1, 3, 2, 4)
        stacked_grads = stacked_grads.reshape(3, row_count, length, heads_local * HEAD_DIM)
        token_grads = lax.all_to_all(
            stacked_grads, "seq", split_axis=2, concat_axis=3, tiled=True
        ).reshape(3, flat_rows, width)
        grad_project = jnp.concatenate(
            [token_grads[0] * 0.125, token_grads[1], token_grads[2]], axis=1
        )
        grad_qkv = jnp.einsum(
            "td,tc->dc", normed_a, grad_project, preferred_element_type=jnp.float32
        )
        bias_q_grad = jnp.sum(grad_project[:, :width].astype(jnp.float32), axis=0)
        bias_v_grad = jnp.sum(grad_project[:, 2 * width :].astype(jnp.float32), axis=0)
        grad_normed_a = jnp.einsum(
            "tc,dc->td", grad_project, qkv_back, preferred_element_type=jnp.float32
        )
        gain_a_grad = jnp.sum(grad_normed_a * unit_a, axis=0)
        shift_a_grad = jnp.sum(grad_normed_a, axis=0)
        grad_x = grad_middle + norm_back(grad_normed_a, unit_a, inverse_a, gain_a)
        input_grads.append(grad_x.reshape(row_count, tokens_local, width))
        vector_grad = jnp.stack(
            [
                gain_a_grad,
                shift_a_grad,
                bias_q_grad,
                bias_v_grad,
                bias_out_grad,
                gain_b_grad,
                shift_b_grad,
                bias_down_grad,
            ],
            axis=1,
        )
        terms = (grad_qkv, grad_outproj, grad_up, grad_down, vector_grad, bias_up_grad)
        shares = share_gradients(terms)
        totals = shares if totals is None else tuple((a + b for a, b in zip(totals, shares)))
    return (
        jnp.stack(outputs),
        jnp.stack(input_grads),
        totals[0],
        totals[1],
        totals[2],
        totals[3],
        totals[4],
        totals[5],
    )


def solution(mesh):
    in_specs = (
        P(None, "fsdp", "seq", None),
        P(None, "fsdp", None),
        P(None, "fsdp", "seq", None),
        P("fsdp", None),
        P("fsdp", None),
        P("fsdp", None),
        P("fsdp", None),
        P("fsdp", None),
        P("fsdp"),
    )
    out_specs = (
        P(None, "fsdp", "seq", None),
        P(None, "fsdp", "seq", None),
        P("fsdp", None),
        P("fsdp", None),
        P("fsdp", None),
        P("fsdp", None),
        P("fsdp", None),
        P("fsdp"),
    )
    return jax.shard_map(shards, mesh=mesh, in_specs=in_specs, out_specs=out_specs, check_vma=False)
```

profile of v0, /device:TPU:0, one launch (start us, length us, event | category | flops | bytes accessed | tf_op | source)
XLA Modules:
  0.0 2255.7 jit_solution(12753321986323332522)
XLA Ops:
  9.4 28.1 %all-gather = bf16[8,96,8]{1,2,0:T(8,128)(2,1)S(1)} all-gather(bf16[1,96,8]{1,2,0:T(8,128)(2,1)} %bitcast.851), channel_id=1, replica_groups=mesh['fsdp'=8,'seq'=4] {'fsdp'}, dimensions={0}, use_global_device_ids=true | all-gather | bytes 13824 | tf_op jit(solution)/shard_map/all_gather | solution.py:164
  40.9 37.3 %all-gather.7.cloned.1.call-done = bf16[768,2304]{1,0:T(8,128)(2,1)} async-done(((bf16[96,2304]{1,0:T(8,128)(2,1)}), bf16[768,2304]{1,0:T(8,128)(2,1)}) %all-gather.7.cloned.1.call-update) | async-done | bytes 3538960 | tf_op jit(solution)/shard_map/all_gather | solution.py:160
  140.6 21.3 while.101
  187.1 21.0 while.100
  221.7 21.0 while.99
  252.5 26.2 %all-gather.1 = bf16[8,1,384]{2,1,0:T(2,128)(2,1)S(1)} all-gather(bf16[1,1,384]{2,1,0:T(2,128)(2,1)S(1)} %reshape.985), channel_id=1, replica_groups=mesh['fsdp'=8,'seq'=4] {'fsdp'}, dimensions={0}, use_global_device_ids=true | all-gather | bytes 6912 | tf_op jit(solution)/shard_map/all_gather | solution.py:165
  359.5 45.5 %while.104 = (s32[]{:T(128)}, f32[1,3,1024,64]{2,3,1,0:T(8,128)}, f32[1,3,1024,64]{2,3,1,0:T(8,128)}, bf16[2,3,512,64]{2,3,1,0:T(8,128)(2,1)}, s32[2]{0:T(128)S(...) while((s32[]{:T(128)}, f32[1,3,1024,64]{2,3,1,0:T(8,128)}, ...), condition=%wide.region_45.46_spmd.clone, body=%wide.region_42.45_spmd.clone.sunk | while | flops 1027308032 | bytes 110220928 | solution.py:120
  409.5 28.9 %all_to_all.180 = bf16[3,1,1024,192]{3,0,1,2:T(4,128)(2,1)} all-to-all(bf16[3,1,1024,192]{3,0,1,2:T(4,128)(2,1)S(1)} %copy.151), channel_id=1, replica_groups=mesh['fsdp'=8,'seq'=4] {'seq'}, dimensions={2} | all-to-all | bytes 2359296 | tf_op jit(solution)/shard_map/all_to_all | solution.py:255
  469.9 46.2 %while.103 = (s32[]{:T(128)}, f32[1,3,1024,64]{2,3,1,0:T(8,128)}, f32[1,3,1024,64]{2,3,1,0:T(8,128)}, bf16[2,3,512,64]{2,3,1,0:T(8,128)(2,1)}, s32[2]{0:T(128)},...) while((s32[]{:T(128)}, f32[1,3,1024,64]{2,3,1,0:T(8,128)}, ...), condition=%wide.region_37.38_spmd.clone, body=%wide.region_34.37_spmd.clone.sunk | while | flops 1027308032 | bytes 110220928 | solution.py:120
  520.7 29.3 %all_to_all.181 = bf16[3,1,1024,192]{3,0,1,2:T(4,128)(2,1)} all-to-all(bf16[3,1,1024,192]{3,0,1,2:T(4,128)(2,1)S(1)} %copy.143), channel_id=1, replica_groups=mesh['fsdp'=8,'seq'=4] {'seq'}, dimensions={2} | all-to-all | bytes 2359296 | tf_op jit(solution)/shard_map/all_to_all | solution.py:255
  581.5 46.8 %while.102 = (s32[]{:T(128)}, f32[1,3,1024,64]{2,3,1,0:T(8,128)}, f32[1,3,1024,64]{2,3,1,0:T(8,128)}, bf16[2,3,512,64]{2,3,1,0:T(8,128)(2,1)}, s32[2]{0:T(128)},...) while((s32[]{:T(128)}, f32[1,3,1024,64]{2,3,1,0:T(8,128)}, ...), condition=%wide.region_29.30_spmd.clone, body=%wide.region_26.29_spmd.clone.sunk | while | flops 1027308032 | bytes 110220928 | solution.py:120
  632.8 28.9 %all_to_all.182 = bf16[3,1,1024,192]{3,0,1,2:T(4,128)(2,1)} all-to-all(bf16[3,1,1024,192]{3,0,1,2:T(4,128)(2,1)S(1)} %copy.135), channel_id=1, replica_groups=mesh['fsdp'=8,'seq'=4] {'seq'}, dimensions={2} | all-to-all | bytes 2359296 | tf_op jit(solution)/shard_map/all_to_all | solution.py:255
  779.9 29.8 %reduce-scatter.24.cloned.1.call-done = f32[96,2304]{1,0:T(8,128)} async-done(((f32[768,2304]{1,0:T(8,128)}), f32[96,2304]{1,0:T(8,128)}) %reduce-scatter.24.cloned.1.call-update) | async-done | bytes 884752 | tf_op jit(solution)/shard_map/reduce_scatter | solution.py:132
  811.7 129.6 %reduce-scatter.22.cloned.1.call-done = f32[96,2304]{1,0:T(8,128)} async-done(((f32[768,2304]{1,0:T(8,128)}), f32[96,2304]{1,0:T(8,128)}) %reduce-scatter.22.cloned.1.call-update) | async-done | bytes 884752 | tf_op jit(solution)/shard_map/reduce_scatter | solution.py:132
  943.4 164.4 %reduce-scatter.38.cloned.1.call-done = f32[96,3072]{1,0:T(8,128)} async-done(((f32[768,3072]{1,0:T(8,128)}), f32[96,3072]{1,0:T(8,128)}) %reduce-scatter.38.cloned.1.call-update) | async-done | bytes 1179664 | tf_op jit(solution)/shard_map/reduce_scatter | solution.py:134
  1109.9 164.2 %reduce-scatter.36.cloned.1.call-done = f32[96,3072]{1,0:T(8,128)} async-done(((f32[768,3072]{1,0:T(8,128)}), f32[96,3072]{1,0:T(8,128)}) %reduce-scatter.36.cloned.1.call-update) | async-done | bytes 1179664 | tf_op jit(solution)/shard_map/reduce_scatter | solution.py:134
  1276.3 164.5 %reduce-scatter.34.cloned.1.call-done = f32[96,3072]{1,0:T(8,128)} async-done(((f32[768,3072]{1,0:T(8,128)}), f32[96,3072]{1,0:T(8,128)}) %reduce-scatter.34.cloned.1.call-update) | async-done | bytes 1179664 | tf_op jit(solution)/shard_map/reduce_scatter | solution.py:134
  1442.9 164.3 %reduce-scatter.44.cloned.1.call-done = f32[384,768]{1,0:T(8,128)} async-done(((f32[3072,768]{1,0:T(8,128)}), f32[384,768]{1,0:T(8,128)}) %reduce-scatter.44.cloned.1.call-update) | async-done | bytes 1179664 | tf_op jit(solution)/shard_map/reduce_scatter | solution.py:135
  1609.3 164.3 %reduce-scatter.42.cloned.1.call-done = f32[384,768]{1,0:T(8,128)} async-done(((f32[3072,768]{1,0:T(8,128)}), f32[384,768]{1,0:T(8,128)}) %reduce-scatter.42.cloned.1.call-update) | async-done | bytes 1179664 | tf_op jit(solution)/shard_map/reduce_scatter | solution.py:135
  1775.8 164.3 %reduce-scatter.40.cloned.1.call-done = f32[384,768]{1,0:T(8,128)} async-done(((f32[3072,768]{1,0:T(8,128)}), f32[384,768]{1,0:T(8,128)}) %reduce-scatter.40.cloned.1.call-update) | async-done | bytes 1179664 | tf_op jit(solution)/shard_map/reduce_scatter | solution.py:135
  1944.8 36.9 %all-reduce.3 = (bf16[3072]{0:T(1024)(128)(2,1)}, bf16[3072]{0:T(1024)(128)(2,1)}, bf16[3072]{0:T(1024)(128)(2,1)}) all-reduce(f32[3072]{0:T(1024)} %get-tuple-element.1198, f32[3072]{0:T(1024)} %get-tuple-element.1200, f32[3072]{0:T(1024)} %get-tuple-element.1202), channel_id=19, replica_groups=mesh['fsdp'=8,'seq'=4] {'fsdp'}, use_global_device_ids=true, to_apply=%region_109.110.clone | all-reduce | flops 9216 | bytes 55296
  2005.1 63.0 %reduce-scatter.48.cloned.1.call-done = f32[96,8]{1,0:T(8,128)} async-done(((f32[768,8]{1,0:T(8,128)}), f32[96,8]{1,0:T(8,128)}) %reduce-scatter.48.cloned.1.call-update) | async-done | bytes 3088
  2068.9 63.2 %reduce-scatter.46.cloned.1.call-done = f32[96,8]{1,0:T(8,128)} async-done(((f32[768,8]{1,0:T(8,128)}), f32[96,8]{1,0:T(8,128)}) %reduce-scatter.46.cloned.1.call-update) | async-done | bytes 3088
  2140.1 100.8 %all-reduce.8.cloned.1.call-done = (bf16[96,2304]{1,0:T(8,128)(2,1)}, bf16[96,2304]{1,0:T(8,128)(2,1)}, bf16[96,2304]{1,0:T(8,128)(2,1)}, bf16[96,768]{1,0:T(8,1...) async-done(((bf16[96,2304]{1,0:T(8,128)(2,1)}, ...) | async-done | bytes 5308432 | tf_op jit(solution)/shard_map/psum | solution.py:140
  (819 shorter events, 623.0 us)
Async XLA Ops:
  7.2 71.1 %all-gather.7.cloned.1.call-start = ((), (), s32[]{:S(2)}) async-start(), calls=%async_computation.27 | async-start | bytes 3981312 | tf_op jit(solution)/shard_map/all_gather | solution.py:160
  7.9 280.3 %all-gather.9.cloned.1.call-start = ((), (), s32[]{:S(2)}) async-start(), calls=%async_computation.28 | async-start | bytes 1327104 | tf_op jit(solution)/shard_map/all_gather | solution.py:161
  8.7 285.8 %all-gather.11.cloned.1.call-start = ((), (), s32[]{:S(2)}) async-start(), calls=%async_computation.29 | async-start | bytes 5308416 | tf_op jit(solution)/shard_map/all_gather | solution.py:162
  91.7 211.6 %all-gather.13.cloned.1.call-start = ((), (), s32[]{:S(2)}) async-start(), calls=%async_computation.30 | async-start | bytes 5308416 | tf_op jit(solution)/shard_map/all_gather | solution.py:163
  135.4 46.4 %all-to-all-start = ((bf16[3,1,256,768]{2,0,1,3:T(4,128)(2,1)}), bf16[3,1,256,768]{2,0,1,3:T(4,128)(2,1)S(1)}, u32[]{:S(2)}, u32[]{:S(2)}) async-start(bf16[3,1,256,768]{2,0,1,3:T(4,128)(2,1)} %copy.111), calls=%async_computation | async-start | bytes 3145728 | tf_op jit(solution)/shard_map/all_to_all | solution.py:179
  181.8 35.6 %all-to-all-start.5 = ((bf16[4,2,24576]{2,1,0:T(2,128)(2,1)}), bf16[4,2,24576]{2,1,0:T(2,128)(2,1)}, u32[]{:S(2)}, u32[]{:S(2)}) async-start(bf16[4,2,24576]{2,1,0:T(2,128)(2,1)} %reshape.1013), calls=%async_computation.5 | async-start | bytes 786432 | tf_op jit(solution)/shard_map/all_to_all | solution.py:188
  217.4 31.6 %all-to-all-start.3 = ((bf16[4,2,24576]{2,1,0:T(2,128)(2,1)}), bf16[4,2,24576]{2,1,0:T(2,128)(2,1)S(1)}, u32[]{:S(2)}, u32[]{:S(2)}) async-start(bf16[4,2,24576]{2,1,0:T(2,128)(2,1)} %reshape.1015), calls=%async_computation.3 | async-start | bytes 786432 | tf_op jit(solution)/shard_map/all_to_all | solution.py:188
  249.0 37.5 %all-to-all-start.1 = ((bf16[4,2,24576]{2,1,0:T(2,128)(2,1)}), bf16[4,2,24576]{2,1,0:T(2,128)(2,1)S(1)}, u32[]{:S(2)}, u32[]{:S(2)}) async-start(bf16[4,2,24576]{2,1,0:T(2,128)(2,1)} %reshape.1017), calls=%async_computation.1 | async-start | bytes 786432 | tf_op jit(solution)/shard_map/all_to_all | solution.py:188
  252.4 520.5 %reduce-scatter.32.cloned.1.call-start = ((), (), s32[]{:S(2)}) async-start(), calls=%async_computation.36 | async-start | bytes 2654208 | tf_op jit(solution)/shard_map/reduce_scatter | solution.py:133
  335.3 439.3 %reduce-scatter.30.cloned.1.call-start = ((), (), s32[]{:S(2)}) async-start(), calls=%async_computation.35 | async-start | bytes 2654208 | tf_op jit(solution)/shard_map/reduce_scatter | solution.py:133
  349.3 426.9 %reduce-scatter.28.cloned.1.call-start = ((), (), s32[]{:S(2)}) async-start(), calls=%async_computation.34 | async-start | bytes 2654208 | tf_op jit(solution)/shard_map/reduce_scatter | solution.py:133
  351.3 426.7 %reduce-scatter.26.cloned.1.call-start = ((), (), s32[]{:S(2)}) async-start(), calls=%async_computation.33 | async-start | bytes 7962624 | tf_op jit(solution)/shard_map/reduce_scatter | solution.py:132
  459.1 350.6 %reduce-scatter.24.cloned.1.call-start = ((), (), s32[]{:S(2)}) async-start(), calls=%async_computation.32 | async-start | bytes 7962624 | tf_op jit(solution)/shard_map/reduce_scatter | solution.py:132
  570.7 370.7 %reduce-scatter.22.cloned.1.call-start = ((), (), s32[]{:S(2)}) async-start(), calls=%async_computation.31 | async-start | bytes 7962624 | tf_op jit(solution)/shard_map/reduce_scatter | solution.py:132
  671.2 436.5 %reduce-scatter.38.cloned.1.call-start = ((), (), s32[]{:S(2)}) async-start(), calls=%async_computation.39 | async-start | bytes 10616832 | tf_op jit(solution)/shard_map/reduce_scatter | solution.py:134
  679.0 595.1 %reduce-scatter.36.cloned.1.call-start = ((), (), s32[]{:S(2)}) async-start(), calls=%async_computation.38 | async-start | bytes 10616832 | tf_op jit(solution)/shard_map/reduce_scatter | solution.py:134
  686.6 754.1 %reduce-scatter.34.cloned.1.call-start = ((), (), s32[]{:S(2)}) async-start(), calls=%async_computation.37 | async-start | bytes 10616832 | tf_op jit(solution)/shard_map/reduce_scatter | solution.py:134
  694.5 912.7 %reduce-scatter.44.cloned.1.call-start = ((), (), s32[]{:S(2)}) async-start(), calls=%async_computation.42 | async-start | bytes 10616832 | tf_op jit(solution)/shard_map/reduce_scatter | solution.py:135
  702.3 1071.4 %reduce-scatter.42.cloned.1.call-start = ((), (), s32[]{:S(2)}) async-start(), calls=%async_computation.41 | async-start | bytes 10616832 | tf_op jit(solution)/shard_map/reduce_scatter | solution.py:135
  710.1 1230.0 %reduce-scatter.40.cloned.1.call-start = ((), (), s32[]{:S(2)}) async-start(), calls=%async_computation.40 | async-start | bytes 10616832 | tf_op jit(solution)/shard_map/reduce_scatter | solution.py:135
  718.3 1286.0 %reduce-scatter.50.cloned.1.call-start = ((), (), s32[]{:S(2)}) async-start(), calls=%async_computation.45 | async-start | bytes 442368
  756.1 1311.9 %reduce-scatter.48.cloned.1.call-start = ((), (), s32[]{:S(2)}) async-start(), calls=%async_computation.44 | async-start | bytes 442368
  762.6 1369.5 %reduce-scatter.46.cloned.1.call-start = ((), (), s32[]{:S(2)}) async-start(), calls=%async_computation.43 | async-start | bytes 442368
  766.5 1474.3 %all-reduce.8.cloned.1.call-start = ((), (), s32[]{:S(2)}) async-start(), calls=%async_computation.46 | async-start | bytes 10616832 | tf_op jit(solution)/shard_map/psum | solution.py:140
  (195 other events, 2048.0 us)
Sparse Core Ops, SparseCore 0:
  10.2 68.0 all-gather.6
  80.4 39.5 all-gather.8
  122.2 78.6 all-gather.10
  202.9 78.2 all-gather.12
  335.4 66.9 reduce-scatter.31
  405.8 68.1 reduce-scatter.29
  477.5 68.1 reduce-scatter.27
  549.4 128.0 reduce-scatter.25
  681.6 128.1 reduce-scatter.23
  813.3 128.0 reduce-scatter.21
  945.4 162.3 reduce-scatter.37
  1111.7 162.3 reduce-scatter.35
  1278.1 162.5 reduce-scatter.33
  1444.6 162.5 reduce-scatter.43
  1611.0 162.5 reduce-scatter.41
  1777.5 162.5 reduce-scatter.39
  1943.6 60.5 reduce-scatter.49
  2007.7 60.3 reduce-scatter.47
  2071.7 60.3 reduce-scatter.45
  2136.1 104.6 all-reduce.7
where the time goes:
time: 2270 us; the launch traced here: 2260 us
  waiting for transfers between devices  1470 us (65%)
  matrix products  259 us (11%)
  blocking collectives  184 us (8%)
  local copies, waits for them, and re-layouts  150 us (7%)
  other arithmetic  117 us (5%)
  starting transfers between devices  34.7 us (2%)
  loops' own time  27.1 us (1%)
    reduce_scatter x3, waiting for transfers between devices, share_gradients(): lax.psum_scatter(terms[2], 'fsdp', scatter_dimension=0, tiled=True)  493 us
    reduce_scatter x3, waiting for transfers between devices, share_gradients(): lax.psum_scatter(terms[3], 'fsdp', scatter_dimension=0, tiled=True)  493 us
    reduce_scatter x3, waiting for transfers between devices, share_gradients(): lax.psum_scatter(terms[0], 'fsdp', scatter_dimension=0, tiled=True)  159 us
    unnamed x23, waiting for transfers between devices  139 us
    psum x1, waiting for transfers between devices, share_gradients(): lax.psum(shares[0].astype(jnp.bfloat16), 'seq').astype(jnp.float32)  101 us
    all_to_all x3, blocking collectives, shards(): lax.all_to_all(stacked_grads, 'seq', split_axis=2, concat_axis=3, tiled=T...  87.2 us
  transfers between devices with their start and end apart: 29, of which 18 were waited for; matrix products, arithmetic and copies ran while one was open for 21% of the time, Pallas kernels for 0%

commit v1 on v0

v1 whole, which is shorter than its diff:
```python
import functools
import math

import jax
import jax.numpy as jnp
from jax import lax
from jax.experimental import pallas as pl
from jax.experimental.pallas import tpu as pltpu
from jax.sharding import PartitionSpec as P

HEADS = 12
HEAD_DIM = 64
EPS = 1e-05
MASKED = -1e30
GELU_A = math.sqrt(2.0 / math.pi)
GELU_B = 0.044715
BF = jnp.bfloat16
F32 = jnp.float32
VMEM_LIMIT = 60 * 1024 * 1024


def shape(dims, dtype=BF):
    return jax.ShapeDtypeStruct(dims, dtype)


def vmem():
    return pl.BlockSpec(memory_space=pltpu.VMEM)


def smem():
    return pl.BlockSpec(memory_space=pltpu.SMEM)


def anywhere():
    return pl.BlockSpec(memory_space=pl.ANY)


def local_kernel(body, outs, name, flops=0, bytes_moved=0, exps=0, **kw):
    return pl.pallas_call(
        body,
        out_shape=outs,
        name=name,
        compiler_params=pltpu.CompilerParams(vmem_limit_bytes=VMEM_LIMIT),
        cost_estimate=pl.CostEstimate(
            flops=flops, bytes_accessed=bytes_moved, transcendentals=exps
        ),
        **kw,
    )


def mm(a, b):
    return lax.dot_general(a, b, (((1,), (0,)), ((), ())), preferred_element_type=F32)


def mm_nt(a, b):
    return lax.dot_general(a, b, (((1,), (1,)), ((), ())), preferred_element_type=F32)


def mm_tn(a, b):
    return lax.dot_general(a, b, (((0,), (0,)), ((), ())), preferred_element_type=F32)


def unit_rows(v):
    centred = v - jnp.mean(v, axis=-1, keepdims=True)
    inverse = lax.rsqrt(jnp.mean(centred * centred, axis=-1, keepdims=True) + EPS)
    return centred * inverse, inverse


def norm_back(grad, unit, inverse, gain):
    t = grad * gain
    first = jnp.mean(t, axis=-1, keepdims=True)
    second = jnp.mean(t * unit, axis=-1, keepdims=True)
    return inverse * (t - first - unit * second)


def pick(at, options):
    out = options[0]
    for s in range(1, len(options)):
        out = jnp.where(at == s, options[s], out)
    return out


def column_of(row, rows):
    return jnp.broadcast_to(row, (128, rows)).T[:, 0:1]


def prep_body(at_ref, wq_ref, up_ref, down_ref, extra_ref, qkv_ref, mlp_ref):
    rows = wq_ref.shape[0]
    width = up_ref.shape[1] // 4
    hw = wq_ref.shape[1] // 12
    part = down_ref.shape[0] // 4
    for s in range(4):

        @pl.when(at_ref[0] == s)
        def _(s=s):
            for n in range(3):
                base = n * 4 * hw + s * hw
                qkv_ref[:, n * hw : (n + 1) * hw] = wq_ref[:, base : base + hw]
            for i in range(width // part):
                col = i * 4 * part + s * part
                mlp_ref[0:rows, i * part : (i + 1) * part] = up_ref[:, col : col + part]
            mlp_ref[rows : rows + part, :] = down_ref[s * part : (s + 1) * part, :]

    qkv_ref[:, 3 * hw :] = extra_ref[...]


def place_body(count, at_ref, *refs):
    pieces, out, sems = refs[:count], refs[count], refs[count + 1]
    copies = [
        pltpu.make_async_copy(piece, out.at[at_ref[n]], sems.at[n])
        for n, piece in enumerate(pieces)
    ]
    for c in copies:
        c.start()
    for c in copies:
        c.wait()


def place(where, pieces, slots):
    return local_kernel(
        functools.partial(place_body, len(pieces)),
        shape((slots,) + pieces[0].shape),
        "place",
        bytes_moved=4 * slots * pieces[0].size,
        in_specs=[smem()] + [anywhere()] * len(pieces),
        out_specs=anywhere(),
        scratch_shapes=[pltpu.SemaphoreType.DMA((len(pieces),))],
    )(where, *pieces)


def segment_column(seg_ref, at, ranks):
    cols = []
    for k in range(4):
        row = seg_ref[pl.ds(ranks[k], 1), :].astype(F32)
        cols.append(column_of(row, row.shape[1]))
    return jnp.concatenate(cols, axis=0)


def forward_body(
    at_ref, x0, x1, x2, x3, w_ref, seg_ref,
    n1_ref, q_ref, k_ref, kt_ref, v_ref, c0, c1, c2, c3, lse_ref, vt_ref, vtr_ref,
):
    at = at_ref[0]
    ranks = [at ^ k for k in range(4)]
    tokens, width = x0.shape
    hw = q_ref.shape[1]
    heads = hw // HEAD_DIM
    tail = (3 * hw) // 128 * 128
    off = 3 * hw - tail
    vt_ref[...] = w_ref[:, tail : tail + 128].astype(F32).T[off : off + 16]
    g1, s1 = vt_ref[0:1, :], vt_ref[1:2, :]
    bq = pick(at, [vt_ref[2:3, s * hw : (s + 1) * hw] for s in range(4)])
    bv = pick(at, [vt_ref[3:4, s * hw : (s + 1) * hw] for s in range(4)])
    for k, x_ref in enumerate((x0, x1, x2, x3)):
        rows = slice(k * tokens, (k + 1) * tokens)
        unit, _ = unit_rows(x_ref[...].astype(F32))
        normed = (unit * g1 + s1).astype(BF)
        n1_ref[rows, :] = normed
        project = mm(normed, w_ref[:, : 3 * hw])
        q_ref[rows, :] = ((project[:, :hw] + bq) * 0.125).astype(BF)
        keys = project[:, hw : 2 * hw]
        k_ref[rows, :] = keys.astype(BF)
        kt_ref[:, rows] = keys.T.astype(BF)
        values = project[:, 2 * hw : 3 * hw] + bv
        v_ref[rows, :] = values.astype(BF)
        vtr_ref[:, rows] = values.T.astype(BF)
    seg_col = segment_column(seg_ref, at, ranks)
    lane_head = lax.broadcasted_iota(jnp.int32, (1, hw), 1) // HEAD_DIM
    lse_ref[...] = jnp.zeros(lse_ref.shape, F32)
    for b, c_ref in enumerate((c0, c1, c2, c3)):
        cols = slice(b * tokens, (b + 1) * tokens)
        seg_row = seg_ref[pl.ds(ranks[b], 1), :].astype(F32)
        bias = jnp.where(seg_col == seg_row, 0.0, MASKED)
        for h in range(heads):
            qh = jnp.where(lane_head == h, q_ref[cols, :], 0).astype(BF)
            s = mm_nt(k_ref[...], qh) + bias
            top = jnp.max(s, axis=0, keepdims=True)
            e = jnp.exp(s - top)
            total = jnp.sum(e, axis=0, keepdims=True)
            part = slice(h * HEAD_DIM, (h + 1) * HEAD_DIM)
            context = mm(vtr_ref[part, :], e.astype(BF)) * (1.0 / total)
            c_ref[part, :] = context.astype(BF)
            lse_ref[h : h + 1, cols] = top + jnp.log(total)


def forward(at, xs, w, seg):
    tokens, width = xs[0].shape
    hw = width // 4
    length = 4 * tokens
    outs = (
        shape((length, width)),
        shape((length, hw)),
        shape((length, hw)),
        shape((hw, length)),
        shape((length, hw)),
        *(shape((hw, tokens)),) * 4,
        shape((8, length), F32),
        shape((16, width), F32),
    )
    flops = 2 * length * width * 3 * hw + 16 * length * length * hw
    return local_kernel(
        forward_body, outs, "attention_forward", flops, 4 * length * width * 2, 3 * length * length,
        in_specs=[smem()] + [vmem()] * 6,
        out_specs=(vmem(),) * len(outs),
        scratch_shapes=[pltpu.VMEM((hw, length), BF)],
    )(at, *xs, w, seg)


def middle_body(at_ref, c0, c1, c2, c3, x_ref, w_ref, vt_ref, y_ref, n2_ref):
    at = at_ref[0]
    hw = c0.shape[0]
    y = x_ref[...].astype(F32) + vt_ref[4:5, :]
    for k, c_ref in enumerate((c0, c1, c2, c3)):
        base = pl.multiple_of((at ^ k) * hw, 64)
        y = y + mm_tn(c_ref[...], w_ref[pl.ds(base, hw), :])
    y_ref[...] = y
    unit, _ = unit_rows(y)
    n2_ref[...] = (unit * vt_ref[5:6, :] + vt_ref[6:7, :]).astype(BF)


def middle(at, cs, x, w_out, vt):
    outs = (shape(x.shape, F32), shape(x.shape))
    return local_kernel(
        middle_body, outs, "middle", 2 * x.size * x.shape[1], 6 * x.size * 2, 0,
        in_specs=[smem()] + [vmem()] * 7,
        out_specs=(vmem(), vmem()),
    )(at, *cs, x, w_out, vt)


def mlp_body(fast, first, micros, at_ref, *refs):
    refs = list(refs)
    take = lambda n: [refs.pop(0) for _ in range(n)]
    n2_refs = take(micros)
    dz_ref, vt_ref = take(2)
    weights = take(4)
    z_in, dn_in = (None, None) if first else take(2)
    z_ref, dn_ref = take(2)
    grads = take(4)
    (bias_ref,) = take(1)
    wu_s, wd_s, n2_s, n2t_s, sem_u, sem_d = take(6)
    step = pl.program_id(0)
    chunk, half = step // 2, step % 2
    width = n2_s.shape[1]
    tokens = n2_s.shape[0] // micros
    hf = wd_s.shape[1]
    y = at_ref[1]

    @pl.when(step == 0)
    def _():
        for t in range(4):
            ch, hh = t // 2, t % 2
            if fast:
                rows = weights[0].shape[1] // 2
                nz = weights[0].shape[0]
                for side in range(2):
                    src = weights[2 * ch + side]
                    yy = y if side == 0 else 1 - y
                    for z in range(nz):
                        dest = pl.multiple_of((2 * z + yy) * rows, 16)
                        pltpu.make_async_copy(
                            src.at[z, pl.ds(0, rows), pl.ds(hh * hf, hf)],
                            wu_s.at[t, pl.ds(dest, rows), :],
                            sem_u.at[t],
                        ).start()
                    for z in range(hh * nz // 2, (hh + 1) * nz // 2):
                        dest = pl.multiple_of((2 * z + yy) * rows - hh * hf, 16)
                        pltpu.make_async_copy(
                            src.at[z, pl.ds(rows, rows), :],
                            wd_s.at[t, pl.ds(dest, rows), :],
                            sem_d.at[t],
                        ).start()
            else:
                pltpu.make_async_copy(
                    weights[2 * ch].at[:, pl.ds(hh * hf, hf)], wu_s.at[t], sem_u.at[t]
                ).start()
                pltpu.make_async_copy(
                    weights[2 * ch + 1].at[pl.ds(hh * hf, hf), :], wd_s.at[t], sem_d.at[t]
                ).start()
        for m in range(micros):
            n2_s[m * tokens : (m + 1) * tokens, :] = n2_refs[m][...]
        n2t_s[...] = n2_s[...].T
        bias_ref[...] = jnp.zeros(bias_ref.shape, F32)
        if first:
            z_ref[...] = jnp.zeros(z_ref.shape, F32)
            dn_ref[...] = jnp.zeros(dn_ref.shape, F32)
        else:
            z_ref[...] = z_in[...]
            dn_ref[...] = dn_in[...]

    pltpu.make_async_copy(wu_s.at[step], wu_s.at[step], sem_u.at[step]).wait()
    pltpu.make_async_copy(wd_s.at[step], wd_s.at[step], sem_d.at[step]).wait()
    wu, wd = wu_s[step], wd_s[step]
    lead = at_ref[2] + chunk
    lanes = pl.ds(pl.multiple_of(half * hf, 128), hf)
    bias = vt_ref[pl.ds(8 + (at_ref[0] ^ lead), 1), lanes]
    u = mm(n2_s[...], wu) + bias
    square = u * u
    t = jnp.tanh(GELU_A * u * (1.0 + GELU_B * square))
    f = (0.5 * u * (1.0 + t)).astype(BF)
    slope = 0.5 * (1.0 + t) + (0.5 * GELU_A) * u * (1.0 - t * t) * (1.0 + 3.0 * GELU_B * square)
    dz = dz_ref[...]
    z_ref[...] += mm(f, wd)
    du = (mm_nt(dz, wd) * slope).astype(BF)
    dn_ref[...] += mm_nt(du, wu)
    bias_ref[pl.ds(chunk, 1), lanes] = jnp.sum(du.astype(F32), axis=0, keepdims=True)
    grad_up = mm(n2t_s[...], du).astype(BF)
    grad_down = mm_tn(f, dz).astype(BF)
    for ch in range(2):
        for hh in range(2):

            @pl.when(step == 2 * ch + hh)
            def _(ch=ch, hh=hh):
                span = slice(hh * hf, (hh + 1) * hf)
                if not fast:
                    grads[2 * ch][:, span] = grad_up
                    grads[2 * ch + 1][span, :] = grad_down
                    return
                rows = grads[0].shape[1] // 2
                count = 2 * grads[0].shape[0]
                for yy in range(2):

                    @pl.when(y == yy)
                    def _(yy=yy):
                        for i in range(count):
                            out = grads[2 * ch + (i % 2 != yy)]
                            out[i // 2, 0:rows, span] = grad_up[i * rows : (i + 1) * rows]
                        for n in range(count // 2):
                            i = hh * count // 2 + n
                            out = grads[2 * ch + (i % 2 != yy)]
                            out[i // 2, rows : 2 * rows, :] = grad_down[n * rows : (n + 1) * rows]


def mlp(fast, info, n2s, dz, vt, weights, carried):
    first = carried is None
    tokens, width = dz.shape
    hf = width // 2
    acc = shape((tokens, width), F32)
    outs = (acc, acc, *(shape(w.shape) for w in weights), shape((8, width), F32))
    ins = (info, *n2s, dz, vt, *weights, *(() if first else carried))
    whole = lambda dims: pl.BlockSpec(dims, lambda i: (0,) * len(dims))
    specs = [smem()] + [whole(a.shape) for a in (*n2s, dz, vt)] + [anywhere()] * 4
    specs += [] if first else [whole(a.shape) for a in carried]
    return local_kernel(
        functools.partial(mlp_body, fast, first, len(n2s)), outs, "feed_forward",
        4 * 12 * tokens * width * hf, 30 * tokens * width, 4 * tokens * hf,
        grid=(4,),
        in_specs=specs,
        out_specs=tuple(whole(o.shape) for o in outs),
        scratch_shapes=[
            pltpu.VMEM((4, width, hf), BF),
            pltpu.VMEM((4, hf, width), BF),
            pltpu.VMEM((tokens, width), BF),
            pltpu.VMEM((width, tokens), BF),
            pltpu.SemaphoreType.DMA((4,)),
            pltpu.SemaphoreType.DMA((4,)),
        ],
    )(*ins)


def turn_body(
    at_ref, y_ref, z_ref, dn_ref, dz_ref, w_ref, vt_ref,
    result_ref, dy_ref, da_ref, d0, d1, d2, d3, sums_ref,
):
    at = at_ref[0]
    hw = d0.shape[0]
    y = y_ref[...]
    result_ref[...] = (y + z_ref[...] + vt_ref[7:8, :]).astype(BF)
    unit, inverse = unit_rows(y)
    dz = dz_ref[...].astype(F32)
    dn = dn_ref[...]
    dy = dz + norm_back(dn, unit, inverse, vt_ref[5:6, :])
    dy_ref[...] = dy
    da = dy.astype(BF)
    da_ref[...] = da
    for k, d_ref in enumerate((d0, d1, d2, d3)):
        base = pl.multiple_of((at ^ k) * hw, 64)
        d_ref[...] = mm_nt(w_ref[pl.ds(base, hw), :], da).astype(BF)
    total = lambda a: jnp.sum(a, axis=0, keepdims=True)
    sums_ref[...] = jnp.concatenate(
        [total(da.astype(F32)), total(dn * unit), total(dn), total(dz), jnp.zeros((4, y.shape[1]), F32)], axis=0
    )


def turn(at, micro, y, z, dn, dz, w_out, vt):
    tokens, width = y.shape
    hw = width // 4
    block = pl.BlockSpec((tokens, width), lambda i: (micro, 0))
    whole = lambda dims: pl.BlockSpec(dims, lambda i: (0,) * len(dims))
    outs = (
        shape((tokens, width)),
        shape((tokens, width), F32),
        shape((tokens, width)),
        *(shape((hw, tokens)),) * 4,
        shape((8, width), F32),
    )
    return local_kernel(
        turn_body, outs, "turn", 2 * tokens * width * width, 20 * tokens * width, 0,
        grid=(1,),
        in_specs=[smem(), whole(y.shape), block, block, block, whole(w_out.shape), whole(vt.shape)],
        out_specs=tuple(whole(o.shape) for o in outs),
    )(at, y, z, dn, dz, w_out, vt)


def outproj_body(fast, micros, info_ref, *refs):
    refs = list(refs)
    cs = [[refs.pop(0) for _ in range(4)] for _ in range(micros)]
    das = [refs.pop(0) for _ in range(micros)]
    outs, scratch = refs[:-1], refs[-1]
    hw = cs[0][0].shape[0]
    at, y = info_ref[0], info_ref[1]
    da = jnp.concatenate([d[...] for d in das], axis=0)
    for k in range(4):
        left = jnp.concatenate([cs[m][k][...] for m in range(micros)], axis=1)
        base = pl.multiple_of((at ^ k) * hw, 64)
        scratch[pl.ds(base, hw), :] = mm(left, da)
    if not fast:
        outs[0][...] = scratch[...]
        return
    keep, keep_other, send = outs
    nz, part = keep.shape[0], keep.shape[1]
    core = at % 2
    for z in range(nz):
        for n in range(2):
            i = 2 * z + (y if n == 0 else 1 - y)
            base = i * 2 * part
            mine = pl.multiple_of(base + core * part, 16)
            others = pl.multiple_of(base + (1 - core) * part, 16)
            (keep, keep_other)[n][z] = scratch[pl.ds(mine, part), :].astype(BF)
            send[n, z] = scratch[pl.ds(others, part), :].astype(BF)


def outproj_grad(fast, info, cs, das, nz, part):
    hw, tokens = cs[0][0].shape
    width = das[0].shape[1]
    micros = len(das)
    if fast:
        one = shape((nz, part, width))
        outs = (one, one, shape((2, nz, part, width)))
    else:
        outs = (shape((width, width), F32),)
    return local_kernel(
        functools.partial(outproj_body, fast, micros), outs, "outproj_grad",
        2 * micros * tokens * width * width, 6 * width * width, 0,
        in_specs=[smem()] + [vmem()] * (5 * micros),
        out_specs=(vmem(),) * len(outs),
        scratch_shapes=[pltpu.VMEM((width, width), F32)],
    )(info, *(c for group in cs for c in group), *das)


def backward_body(first, at_ref, *refs):
    refs = list(refs)
    take = lambda n: [refs.pop(0) for _ in range(n)]
    ds, cs, xs = take(4), take(4), take(4)
    q_ref, k_ref, kt_ref, v_ref, lse_ref, seg_ref, w_ref, n1_ref, vt_ref = take(9)
    acc_in, sums_in = (None, None) if first else take(2)
    acc_ref, sums_ref, dn0_ref, dn2_ref, dn13_ref = take(5)
    dk_s, dv_s, dp_s = take(3)
    at = at_ref[0]
    ranks = [at ^ k for k in range(4)]
    hw, tokens = ds[0].shape
    heads = hw // HEAD_DIM
    seg_col = segment_column(seg_ref, at, ranks)
    lane_head = lax.broadcasted_iota(jnp.int32, (1, hw), 1) // HEAD_DIM
    for b in range(4):
        rows = slice(b * tokens, (b + 1) * tokens)
        seg_row = seg_ref[pl.ds(ranks[b], 1), :].astype(F32)
        bias = jnp.where(seg_col == seg_row, 0.0, MASKED)
        dct = ds[b][...]
        dc = dct.T
        product = dct.astype(F32) * cs[b][...].astype(F32)
        grads, probs, queries, contexts, dqs = [], [], [], [], []
        for h in range(heads):
            part = slice(h * HEAD_DIM, (h + 1) * HEAD_DIM)
            qh = jnp.where(lane_head == h, q_ref[rows, :], 0).astype(BF)
            dch = jnp.where(lane_head == h, dc, 0).astype(BF)
            p = jnp.exp(mm_nt(k_ref[...], qh) + bias - lse_ref[h : h + 1, rows])
            delta = jnp.sum(product[part], axis=0, keepdims=True)
            g = (p * (mm_nt(v_ref[...], dch) - delta)).astype(BF)
            grads.append(g)
            probs.append(p.astype(BF))
            queries.append(qh)
            contexts.append(dch)
            dqs.append(mm(kt_ref[part, :], g))
        dk = mm(jnp.concatenate(grads, axis=1), jnp.concatenate(queries, axis=0))
        dv = mm(jnp.concatenate(probs, axis=1), jnp.concatenate(contexts, axis=0))
        if b == 0:
            dk_s[...] = dk
            dv_s[...] = dv
        else:
            dk_s[...] += dk
            dv_s[...] += dv
        dq = jnp.concatenate(dqs, axis=0).T.astype(BF)
        dp_s[rows, 0:hw] = (dq.astype(F32) * 0.125).astype(BF)
    dp_s[:, hw : 2 * hw] = dk_s[...].astype(BF)
    dp_s[:, 2 * hw : 3 * hw] = dv_s[...].astype(BF)
    total = lambda a: jnp.sum(a, axis=0, keepdims=True)
    acc = mm_tn(n1_ref[...], dp_s[...])
    acc_ref[...] = acc if first else acc_in[...] + acc
    dg1 = ds1 = None
    outs = ((dn0_ref, 0), (dn13_ref, 0), (dn2_ref, 0), (dn13_ref, tokens))
    for k in range(4):
        rows = slice(k * tokens, (k + 1) * tokens)
        dn1 = mm_nt(dp_s[rows, :], w_ref[:, : 3 * hw])
        unit, _ = unit_rows(xs[k][...].astype(F32))
        a, b = total(dn1 * unit), total(dn1)
        dg1, ds1 = (a, b) if k == 0 else (dg1 + a, ds1 + b)
        ref, base = outs[k]
        ref[base : base + tokens, :] = dn1.astype(BF)
    dbq, dbv = (total(dp_s[:, n * hw : (n + 1) * hw].astype(F32)) for n in (0, 2))
    spread = lambda r: jnp.concatenate([jnp.where(at == s, r, 0.0) for s in range(4)], axis=1)
    sums = jnp.concatenate([dg1, ds1, spread(dbq), spread(dbv), jnp.zeros((4, dg1.shape[1]), F32)], axis=0)
    sums_ref[...] = sums if first else sums_in[...] + sums


def backward(at, ds, cs, xs, kept, seg, w, vt, carried):
    n1, q, k, kt, v, lse = kept
    hw, tokens = ds[0].shape
    length, width = n1.shape
    first = carried is None
    outs = (
        shape((width, 3 * hw), F32),
        shape((8, width), F32),
        shape((tokens, width)),
        shape((tokens, width)),
        shape((2 * tokens, width)),
    )
    ins = (*ds, *cs, *xs, q, k, kt, v, lse, seg, w, n1, vt, *(() if first else carried))
    flops = 4 * length * width * 3 * hw + 40 * length * length * hw
    return local_kernel(
        functools.partial(backward_body, first), outs, "attention_backward",
        flops, 8 * length * width * 2, 3 * length * length,
        in_specs=[smem()] + [vmem()] * len(ins),
        out_specs=(vmem(),) * len(outs),
        scratch_shapes=[
            pltpu.VMEM((length, hw), F32),
            pltpu.VMEM((length, hw), F32),
            pltpu.VMEM((length, 3 * hw), BF),
        ],
    )(at, *ins)


def finish_body(a_ref, b_ref, dy_ref, x_ref, vt_ref, gx_ref):
    unit, inverse = unit_rows(x_ref[...].astype(F32))
    dn1 = a_ref[...].astype(F32) + b_ref[...].astype(F32)
    gx_ref[...] = dy_ref[...] + norm_back(dn1, unit, inverse, vt_ref[0:1, :])


def finish(a, b, dy, x, vt):
    return local_kernel(
        finish_body, shape(x.shape, F32), "finish", 20 * x.size, 12 * x.size, 0,
        in_specs=[vmem()] * 5,
        out_specs=vmem(),
    )(a, b, dy, x, vt)


def pack_body(fast, info_ref, acc_ref, rows_ref, *outs):
    width = acc_ref.shape[0]
    hw3 = acc_ref.shape[1]
    columns = jnp.concatenate([rows_ref[...], jnp.zeros((112, width), F32)], axis=0).T[:, 0:64]
    full = jnp.concatenate([acc_ref[...], columns], axis=1)
    if not fast:
        outs[0][...] = full
        return
    own, other = outs
    nz, part = own.shape[0], own.shape[1]
    for y in range(2):

        @pl.when(info_ref[1] == y)
        def _(y=y):
            for i in range(2 * nz):
                out = own if i % 2 == y else other
                out[i // 2] = full[i * part : (i + 1) * part].astype(BF)


def pack(fast, info, acc, rows, nz, part):
    width = acc.shape[0]
    cols = acc.shape[1] + 64
    if fast:
        outs = (shape((nz, part, cols)),) * 2
    else:
        outs = (shape((width, cols), F32),)
    return local_kernel(
        functools.partial(pack_body, fast), outs, "pack", 0, 6 * width * cols, 0,
        in_specs=[smem(), vmem(), vmem()],
        out_specs=(vmem(),) * len(outs),
    )(info, acc, rows)


def assemble_body(
    at_ref, m0, m1, m2, m3, q0, q1, q2, q3, o0, o1,
    gq_ref, go_ref, gu_ref, gd_ref, ex_ref, ms, qs,
):
    at = at_ref[0]
    for k, r in enumerate((m0, m1, m2, m3)):
        ms[at ^ k] = r[...]
    for k, r in enumerate((q0, q1, q2, q3)):
        qs[at ^ k] = r[...].astype(F32)
    rows, part = gu_ref.shape[0], gd_ref.shape[0] // 4
    hw = gq_ref.shape[1] // 12
    for s in range(4):
        up = ms[s, 0:rows, :].astype(F32)
        for i in range(up.shape[1] // part):
            col = i * 4 * part + s * part
            gu_ref[:, col : col + part] = up[:, i * part : (i + 1) * part]
        gd_ref[s * part : (s + 1) * part, :] = ms[s, rows : rows + part, :].astype(F32)
        for n in range(3):
            base = n * 4 * hw + s * hw
            gq_ref[:, base : base + hw] = qs[s, :, n * hw : (n + 1) * hw]
    ex_ref[...] = (qs[0] + qs[1] + qs[2] + qs[3])[:, 3 * hw :]
    first = at % 2 == 0
    a, b = o0[...].astype(F32), o1[...].astype(F32)
    half = a.shape[0]
    go_ref[0:half, :] = jnp.where(first, a, b)
    go_ref[half : 2 * half, :] = jnp.where(first, b, a)


def assemble(at, ms, qs, os, ff):
    width = ms[0].shape[1]
    rows, cols = qs[0].shape
    part = ms[0].shape[0] - rows
    hw = (cols - 64) // 3
    outs = (
        shape((rows, 12 * hw), F32),
        shape((rows, width), F32),
        shape((rows, 4 * width), F32),
        shape((4 * part, width), F32),
        shape((rows, 64), F32),
    )
    return local_kernel(
        assemble_body, outs, "assemble", 0, 16 * rows * width * 4, 0,
        in_specs=[smem()] + [vmem()] * 10,
        out_specs=(vmem(),) * len(outs),
        scratch_shapes=[
            pltpu.VMEM((4,) + ms[0].shape, BF),
            pltpu.VMEM((4,) + qs[0].shape, F32),
        ],
    )(at, *ms, *qs, *os)


def send(x, axis, to):
    n = lax.axis_size(axis)
    return lax.ppermute(x, axis, [(s, to(s)) for s in range(n)])


def seq_swap(x, k):
    return send(x, "seq", lambda s: s ^ k)


def add(*terms):
    out = terms[0].astype(F32)
    for t in terms[1:]:
        out = out + t.astype(F32)
    return out.astype(BF)


def shards(inputs, segments, cotangent, w_qkv, w_out, w_up, w_down, vectors, bias_up):
    micros, _, tokens, width = inputs.shape
    nf = lax.axis_size("fsdp")
    assert lax.axis_size("seq") == 4 and inputs.shape[1] == 1
    rows = w_qkv.shape[0]
    part = w_down.shape[0] // 4
    hw = width // 4
    nz = nf // 2
    fast = nf == 8 and rows % 32 == 0 and part == rows
    at = lax.axis_index("seq")
    me = lax.axis_index("fsdp")
    z, y = me // 2, me % 2
    at1 = at[None].astype(jnp.int32)
    info = jnp.stack([at, y]).astype(jnp.int32)
    infos = [jnp.stack([at, y, jnp.int32(n)]).astype(jnp.int32) for n in (0, 2)]
    y_swap = lambda x: send(x, "fsdp", lambda s: s ^ 1)
    z_pull = lambda x, d: send(x, "fsdp", lambda s: (s - 2 * d) % nf)

    if fast:
        extra = jnp.concatenate([vectors, bias_up.reshape(4, part).T, jnp.zeros((rows, 52), BF)], axis=1)
        qkv_piece, mlp_piece = local_kernel(
            prep_body, (shape((rows, 3 * hw + 64)), shape((rows + part, width))), "prep",
            0, 6 * rows * 4 * width, 0,
            in_specs=[smem()] + [vmem()] * 4,
            out_specs=(vmem(), vmem()),
        )(at1, w_qkv, w_up, w_down, extra)
        out_piece = lax.dynamic_slice_in_dim(w_out, (at % 2) * (rows // 2), rows // 2, 0)
        zs = [(z + d) % nz for d in range(nz)]
        where_all = jnp.stack([2 * a + y for a in zs] + [2 * a + 1 - y for a in zs]).astype(jnp.int32)
        where_z = jnp.stack(zs).astype(jnp.int32)

        def over_zy(piece):
            pulled = [piece] + [z_pull(piece, d) for d in range(1, nz)]
            return pulled + [y_swap(p) for p in pulled]

        w_heads = place(where_all, over_zy(qkv_piece), nf).reshape(width, 3 * hw + 64)
        half = place(where_all, over_zy(out_piece), nf)
        other = seq_swap(half, 1)
        even = at % 2 == 0
        w_out_full = jnp.stack(
            [jnp.where(even, half, other), jnp.where(even, other, half)], axis=1
        ).reshape(width, width)
        own = place(where_z, [mlp_piece] + [z_pull(mlp_piece, d) for d in range(1, nz)], nz)
        oth = y_swap(own)
        own_x = seq_swap(own, 2)
        oth_x = y_swap(own_x)
        chunks = [
            (own, oth),
            (seq_swap(own, 1), seq_swap(oth, 1)),
            (own_x, oth_x),
            (seq_swap(own_x, 1), seq_swap(oth_x, 1)),
        ]
    else:
        gather = lambda a: lax.all_gather(a, "fsdp", axis=0, tiled=True)
        by_head = gather(w_qkv).reshape(width, 3, 4, hw)
        mine = lax.dynamic_index_in_dim(by_head, at, 2, keepdims=False).reshape(width, 3 * hw)
        biases = gather(bias_up).reshape(nf, 4, part).transpose(0, 2, 1).reshape(width, 4)
        w_heads = jnp.concatenate([mine, gather(vectors), biases, jnp.zeros((width, 52), BF)], axis=1)
        w_out_full = gather(w_out)
        ups = gather(w_up).reshape(width, nf, 4, part).transpose(2, 0, 1, 3).reshape(4, width, width)
        downs = gather(w_down).reshape(nf, 4, part, width).transpose(1, 0, 2, 3).reshape(4, width, width)
        one = lambda a, k: lax.dynamic_index_in_dim(a, at ^ k, 0, keepdims=False)
        chunks = [(one(ups, k), one(downs, k)) for k in range(4)]

    segs = segments[:, 0].reshape(micros, 4, tokens)
    own_x_rows = [inputs[m, 0] for m in range(micros)]
    saved, contexts, ys, n2s, spread = [], [], [], [], []
    vt = None
    for m in range(micros):
        x = own_x_rows[m]
        across = seq_swap(x, 2)
        xs = [x, seq_swap(x, 1), across, seq_swap(across, 1)]
        n1, q, k, kt, v, c0, c1, c2, c3, lse, vt = forward(at1, xs, w_heads, segs[m])
        cs = [c0, c1, c2, c3]
        spread.append((xs, cs))
        saved.append((n1, q, k, kt, v, lse))
        contexts.append([c0] + [seq_swap(cs[k], k) for k in (1, 2, 3)])
    for m in range(micros):
        y_m, n2 = middle(at1, contexts[m], own_x_rows[m], w_out_full, vt)
        ys.append(y_m)
        n2s.append(n2)

    dz = cotangent.reshape(micros * tokens, width)
    za, dna, *grads_a, bias_a = mlp(fast, infos[0], n2s, dz, vt, [*chunks[0], *chunks[1]], None)
    zb, dnb, *grads_b, bias_b = mlp(fast, infos[1], n2s, dz, vt, [*chunks[2], *chunks[3]], (za, dna))

    results, dys, das, dcs, row_sums = [], [], [], [], []
    for m in range(micros):
        result, dy, da, d0, d1, d2, d3, sums = turn(at1, m, ys[m], zb, dnb, dz, w_out_full, vt)
        results.append(result)
        dys.append(dy)
        das.append(da)
        row_sums.append(sums)
        dcs.append([d0, seq_swap(d1, 1), seq_swap(d2, 2), seq_swap(d3, 3)])
    out_grads = outproj_grad(fast, info, contexts, das, nz, rows // 2)
    carried = None
    grad_rows = []
    for m in range(micros):
        xs, cs = spread[m]
        acc, sums, dn0, dn2, dn13 = backward(
            at1, dcs[m], cs, xs, saved[m], segs[m], w_heads, vt, carried
        )
        carried = (acc, sums)
        got = seq_swap(dn13, 1)
        mine = add(dn0, got[:tokens])
        theirs = seq_swap(add(dn2, got[tokens:]), 2)
        grad_rows.append(finish(mine, theirs, dys[m], own_x_rows[m], vt))
    acc, sums = carried
    sums_turn = functools.reduce(jnp.add, row_sums)
    bias_rel = jnp.concatenate([bias_a[:2], bias_b[:2]], axis=0)
    bias_abs = jnp.stack(
        [lax.dynamic_index_in_dim(bias_rel, at ^ s, 0, keepdims=False) for s in range(4)]
    )
    rows16 = jnp.concatenate([sums[:4], sums_turn[:4], bias_abs, jnp.zeros((4, width), F32)], axis=0)
    packed = pack(fast, info, acc, rows16, nz, rows)

    if fast:

        def over_z(a):
            return add(
                lax.dynamic_index_in_dim(a, z, 0, keepdims=False),
                *(
                    z_pull(lax.dynamic_index_in_dim(a, (z - d) % nz, 0, keepdims=False), d)
                    for d in range(1, nz)
                ),
            )

        def seq_pieces(a):
            b = seq_swap(a, 2)
            return [a, seq_swap(a, 1), b, seq_swap(b, 1)]

        def chip_sum(k):
            mine, theirs = (grads_a[:2], grads_a[2:]) if k == 0 else (grads_b[:2], grads_b[2:])
            own, oth = (add(a, seq_swap(b, 1)) for a, b in zip(mine, theirs))
            return add(own, y_swap(oth))

        far = chip_sum(2)
        near = chip_sum(0)
        mlp_share = seq_pieces(over_z(add(near, seq_swap(far, 2))))
        keep, keep_other, to_core = out_grads
        from_core = seq_swap(to_core, 1)
        half = add(add(keep, from_core[0]), y_swap(add(keep_other, from_core[1])))
        half = over_z(add(half, seq_swap(half, 2)))
        out_share = [half, seq_swap(half, 1)]
        mine, oth = packed
        qkv_share = seq_pieces(over_z(add(mine, y_swap(oth))))
        g_qkv, g_out, g_up, g_down, g_extra = assemble(at1, mlp_share, qkv_share, out_share, w_up.shape[1])
        g_vec, g_bias = g_extra[:, :8], g_extra[:, 8:12].T.reshape(4 * part)
    else:
        total = lambda a: lax.psum(
            lax.psum_scatter(a.astype(F32), "fsdp", scatter_dimension=0, tiled=True), "seq"
        )
        head_place = lambda a: lax.dynamic_update_slice_in_dim(
            jnp.zeros((width, 3, 4, hw), F32), a.reshape(width, 3, 1, hw), at, 2
        ).reshape(width, 12 * hw)
        full = packed[0]
        g_qkv = total(head_place(full[:, : 3 * hw]))
        g_out = total(out_grads[0])
        extra = total(full[:, 3 * hw :])
        g_vec, g_bias = extra[:, :8], extra[:, 8:12].T.reshape(4 * part)
        pairs = [grads_a[:2], grads_a[2:], grads_b[:2], grads_b[2:]]
        order = lambda n: jnp.stack(
            [
                lax.dynamic_index_in_dim(jnp.stack([p[n] for p in pairs]), at ^ s, 0, keepdims=False)
                for s in range(4)
            ]
        )
        ups = order(0).reshape(4, width, nf, part).transpose(1, 2, 0, 3).reshape(width, 4 * width)
        downs = order(1).reshape(4, nf, part, width).transpose(1, 0, 2, 3).reshape(4 * width, width)
        g_up, g_down = total(ups), total(downs)
    return (
        jnp.stack(results)[:, None],
        jnp.stack(grad_rows)[:, None],
        g_qkv,
        g_out,
        g_up,
        g_down,
        g_vec,
        g_bias,
    )


def solution(mesh):
    rows = P(None, "fsdp", "seq", None)
    first = P("fsdp", None)
    in_specs = (rows, P(None, "fsdp", None), rows, first, first, first, first, first, P("fsdp"))
    out_specs = (rows, rows, first, first, first, first, first, P("fsdp"))
    return jax.shard_map(shards, mesh=mesh, in_specs=in_specs, out_specs=out_specs, check_vma=False)
```

time: 2270 us -> 552 us (0.24)
  waiting for transfers between devices: 1470 us -> 135 us
  Pallas kernels: 0 us -> 272 us
  matrix products: 259 us -> 0 us
  blocking collectives: 184 us -> 0 us
  local copies, waits for them, and re-layouts: 150 us -> 19.3 us
  other arithmetic: 117 us -> 20.6 us
  starting transfers between devices: 34.7 us -> 92.1 us
  loops' own time: 27.1 us -> 0 us
    reduce_scatter x12 -> x0, waiting for transfers between devices: 1150 us -> none  [the longest x3 493 us: share_gradients(): lax.psum_scatter(terms[2], 'fsdp', scatter_dimension=0, tiled=True)]
    pallas_call x0 -> x24, Pallas kernels: none -> 272 us  [the longest x3 89 us: place(): local_kernel(functools.partial(place_body, len(pieces)), shape((slots,) +...]
    dot_general x78 -> x0, matrix products: 259 us -> none  [the longest x6 28 us: one_block(): jnp.einsum('hqk,hqe->hke', probability.astype(jnp.bfloat16), grad_block,...]
    unnamed x23 -> x0, waiting for transfers between devices: 139 us -> none
    ppermute x0 -> x85, waiting for transfers between devices: none -> 135 us  [send(): return lax.ppermute(x, axis, [(s, to(s)) for s in range(n)])]
    psum x1 -> x0, waiting for transfers between devices: 101 us -> none  [share_gradients(): lax.psum(shares[0].astype(jnp.bfloat16), 'seq').astype(jnp.float32)]
    ppermute x0 -> x85, starting transfers between devices: none -> 92.1 us  [send(): return lax.ppermute(x, axis, [(s, to(s)) for s in range(n)])]
    all_to_all x3 -> x0, blocking collectives: 87.2 us -> none  [shards(): lax.all_to_all(stacked_grads, 'seq', split_axis=2, concat_axis=3, tiled=T...]
  transfers between devices with their start and end apart: 29 -> 85, of which waited for: 18 -> 24; matrix products, arithmetic and copies ran while one was open for 21% -> 5% of each run, Pallas kernels for 0% -> 50%
where the time goes in v1:
time: 552 us; the launch traced here: 541 us
  Pallas kernels  272 us (49%)
  waiting for transfers between devices  135 us (24%)
  starting transfers between devices  92.1 us (17%)
  other arithmetic  20.6 us (4%)
  local copies, waits for them, and re-layouts  19.3 us (3%)
    ppermute x85, waiting for transfers between devices, send(): return lax.ppermute(x, axis, [(s, to(s)) for s in range(n)])  135 us
    ppermute x85, starting transfers between devices, send(): return lax.ppermute(x, axis, [(s, to(s)) for s in range(n)])  92.1 us
    pallas_call x3, Pallas kernels, place(): local_kernel(functools.partial(place_body, len(pieces)), shape((slots,) +...  89 us
    pallas_call x3, Pallas kernels, backward(): local_kernel(functools.partial(backward_body, first), outs, 'attention_ba...  50.7 us
    pallas_call x2, Pallas kernels, mlp(): local_kernel(functools.partial(mlp_body, fast, first, len(n2s)), outs, 'f...  47.8 us
    pallas_call x3, Pallas kernels, forward(): local_kernel(forward_body, outs, 'attention_forward', flops, 4 * length *...  40.8 us
    pallas_call x3, Pallas kernels, turn(): local_kernel(turn_body, outs, 'turn', 2 * tokens * width * width, 20 * to...  12.2 us
    convert_element_type x14, other arithmetic, add(): return out.astype(BF)  12 us
  transfers between devices with their start and end apart: 85, of which 24 were waited for; matrix products, arithmetic and copies ran while one was open for 5% of the time, Pallas kernels for 50%

profile of v1, /device:TPU:0, one launch (start us, length us, event | category | flops | bytes accessed | tf_op | source)
XLA Modules:
  0.0 541.2 jit_solution(1043411230897953509)
XLA Ops:
  1.6 5.1 collective-permute-start.13
  23.1 16.0 %collective-permute-start.5 = (bf16[96,640]{1,0:T(8,128)(2,1)S(1)}, bf16[96,640]{1,0:T(8,128)(2,1)S(1)}, u32[]{:S(2)}, u32[]{:S(2)}) collective-permute-start(bf16[96,640]{1,0:T(8,128)(2,1)S(1)} %copy-done.38), channel_id=1, source_target_pairs={{0,8},{4,12},{8,16},{12,20},{16,24},{20,28},{24,0},{28,4},{1,9},{5... | collective-permute-start | bytes 368648 | tf_op jit(solution)/shard_map/ppermute | solution.py:642
  39.1 9.6 %collective-permute-done.34.refs_2_ = bf16[192,768]{1,0:T(8,128)(2,1)S(1)} collective-permute-done((bf16[192,768]{1,0:T(8,128)(2,1)}, bf16[192,768]{1,0:T(8,128)(2,1)S(1)}, u32[]{:S(2)}, u32[]{:S(2)}) %collective-permute-start.34) | collective-permute-done | bytes 294944 | tf_op jit(solution)/shard_map/ppermute | solution.py:642
  51.0 37.7 %place.5.refs_5_ = bf16[4,192,768]{2,1,0:T(8,128)(2,1)} custom-call(s32[4]{0:T(128)} %pad_add_fusion.2.at_ref, bf16[192,768]{1,0:T(8,128)(2,1)} %get-tuple-element.128.refs_0_, bf16[192,768]{1,0:T(8,128)(2,1)} %copy-done.29, bf16[192,768]{1,0:T(8,128)(2,1)} %copy-done.30, bf16[192,768]{1,0:T(8,128)(2,1)} %copy-done.31), custom_call_target="tpu_custom_call" | custom-call | bytes 2359296 | tf_op jit(solution)/shard_map/place/pallas_call | solution.py:120
  107.3 18.9 %collective-permute-done.22.x2.refs_10_ = bf16[256,768]{1,0:T(8,128)(2,1)S(1)} collective-permute-done((bf16[256,768]{1,0:T(8,128)(2,1)S(1)}, bf16[256,768]{1,0:T(8,128)(2,1)S(1)}, u32[]{:S(2)}, u32[]{:S(2)}) %collective-permute-start.22) | collective-permute-done | bytes 393248 | tf_op jit(solution)/shard_map/ppermute | solution.py:642
  127.7 7.0 %collective-permute-done.1.x2.refs_10_ = bf16[256,768]{1,0:T(8,128)(2,1)} collective-permute-done((bf16[256,768]{1,0:T(8,128)(2,1)S(1)}, bf16[256,768]{1,0:T(8,128)(2,1)}, u32[]{:S(2)}, u32[]{:S(2)}) %collective-permute-start.1) | collective-permute-done | bytes 393248 | tf_op jit(solution)/shard_map/ppermute | solution.py:642
  135.4 19.7 %place.4 = bf16[8,48,768]{2,1,0:T(8,128)(2,1)} custom-call(s32[8]{0:T(128)} %stack.104.at_ref, bf16[48,768]{1,0:T(8,128)(2,1)} %copy-done.32, bf16[48,768]{1,0:T(8,128)(2,1)} %copy-done.57, bf16[48,768]{1,0:T(8,128)(2,1)} %copy-done.58, bf16[48,768]{1,0:T(8,128)(2,1)} %copy-done.60, bf16[48,768]{1,0:T(8,128)(2,1)} %collective-permute-done.16.refs_4_, ...), custom_call_target="tpu_custom_call" | custom-call | bytes 1179648 | tf_op jit(solution)/shard_map/place/pallas_call | solution.py:120
  159.3 31.6 %place.3 = bf16[8,96,640]{2,1,0:T(8,128)(2,1)} custom-call(s32[8]{0:T(128)} %stack.104.at_ref, bf16[96,640]{1,0:T(8,128)(2,1)} %get-tuple-element.110.refs_0_, bf16[96,640]{1,0:T(8,128)(2,1)} %collective-permute-done.3.refs_1_, bf16[96,640]{1,0:T(8,128)(2,1)} %copy-done.39, bf16[96,640]{1,0:T(8,128)(2,1)} %copy-done.40, bf16[96,640]{1,0:T(8,128)(2,1)} %copy-done.41, ...), custom_call_target="tpu_custom_call" | custom-call | bytes 1966080 | tf_op jit(solution)/shard_map/place/pallas_call | solution.py:120
  191.5 13.5 %attention_forward.4 = (bf16[1024,768]{1,0:T(8,128)(2,1)}, bf16[1024,192]{1,0:T(8,128)(2,1)}, bf16[1024,192]{1,0:T(8,128)(2,1)}, bf16[192,1024]{1,0:T(8,128)(2,1...) custom-call(s32[1]{0:T(128)} %bitcast.at_ref, ...), custom_call_target="tpu_custom_call" | custom-call | flops 4127195136 | bytes 6291456 | tf_op jit(solution)/shard_map/attention_forward/pallas_call | solution.py:201
  207.1 13.6 %attention_forward.3 = (bf16[1024,768]{1,0:T(8,128)(2,1)}, bf16[1024,192]{1,0:T(8,128)(2,1)}, bf16[1024,192]{1,0:T(8,128)(2,1)}, bf16[192,1024]{1,0:T(8,128)(2,1...) custom-call(s32[1]{0:T(128)} %bitcast.at_ref, ...), custom_call_target="tpu_custom_call" | custom-call | flops 4127195136 | bytes 6291456 | tf_op jit(solution)/shard_map/attention_forward/pallas_call | solution.py:201
  227.0 13.7 %attention_forward.5 = (bf16[1024,768]{1,0:T(8,128)(2,1)}, bf16[1024,192]{1,0:T(8,128)(2,1)}, bf16[1024,192]{1,0:T(8,128)(2,1)}, bf16[192,1024]{1,0:T(8,128)(2,1...) custom-call(s32[1]{0:T(128)} %bitcast.at_ref, ...), custom_call_target="tpu_custom_call" | custom-call | flops 4127195136 | bytes 6291456 | tf_op jit(solution)/shard_map/attention_forward/pallas_call | solution.py:201
  260.0 23.1 %feed_forward.2 = (f32[768,768]{1,0:T(8,128)}, f32[768,768]{1,0:T(8,128)}, bf16[4,192,768]{2,1,0:T(8,128)(2,1)}, bf16[4,192,768]{2,1,0:T(8,128)(2,1)}, bf16[4,19...) custom-call(s32[3]{0:T(128)} %pad_add_fusion.3.at_ref, ...), custom_call_target="tpu_custom_call" | custom-call | flops 10871635968 | bytes 17694720 | tf_op jit(solution)/shard_map/feed_forward/pallas_call | solution.py:343
  284.0 24.7 %feed_forward.3 = (f32[768,768]{1,0:T(8,128)}, f32[768,768]{1,0:T(8,128)}, bf16[4,192,768]{2,1,0:T(8,128)(2,1)}, bf16[4,192,768]{2,1,0:T(8,128)(2,1)}, bf16[4,19...) custom-call(s32[3]{0:T(128)} %pad_add_fusion.at_ref, ...), custom_call_target="tpu_custom_call" | custom-call | flops 10871635968 | bytes 17694720 | tf_op jit(solution)/shard_map/feed_forward/pallas_call | solution.py:343
  334.3 16.7 %attention_backward.3 = (f32[768,576]{1,0:T(8,128)}, f32[8,768]{1,0:T(8,128)}, bf16[256,768]{1,0:T(8,128)(2,1)}, bf16[256,768]{1,0:T(8,128)(2,1)}, bf16[512,768]{1,0:T(8,128)(2,1)}) custom-call(s32[1]{0:T(128)} %bitcast.at_ref, bf16[192,256]{1,0:T(8,128)(2,1)} %get-tuple-element.138.refs_0_, bf16[192,256]{1,0:T(8,128)(2,1)} %copy-done.87, ...), custom_call_target="tpu_custom_call" | custom-call | flops 9865003008 | bytes 12582912 | tf_op jit(solution)/shard_map/attention_backward/pallas_call | solution.py:529
  357.4 16.9 %attention_backward.4 = (f32[768,576]{1,0:T(8,128)}, f32[8,768]{1,0:T(8,128)}, bf16[256,768]{1,0:T(8,128)(2,1)}, bf16[256,768]{1,0:T(8,128)(2,1)}, bf16[512,768]{1,0:T(8,128)(2,1)}) custom-call(s32[1]{0:T(128)} %bitcast.at_ref, bf16[192,256]{1,0:T(8,128)(2,1)} %get-tuple-element.152.refs_0_, bf16[192,256]{1,0:T(8,128)(2,1)} %collective-permute-done.48.refs_1_, ...), custom_call_target="tpu_custom_call" | custom-call | flops 9865003008 | bytes 12582912 | tf_op jit(solution)/shard_map/attention_backward/pallas_call | solution.py:529
  376.4 17.0 %attention_backward.5 = (f32[768,576]{1,0:T(8,128)}, f32[8,768]{1,0:T(8,128)}, bf16[256,768]{1,0:T(8,128)(2,1)}, bf16[256,768]{1,0:T(8,128)(2,1)}, bf16[512,768]{1,0:T(8,128)(2,1)}) custom-call(s32[1]{0:T(128)} %bitcast.at_ref, bf16[192,256]{1,0:T(8,128)(2,1)} %get-tuple-element.168.refs_0_, bf16[192,256]{1,0:T(8,128)(2,1)} %copy-done.82, ...), custom_call_target="tpu_custom_call" | custom-call | flops 9865003008 | bytes 12582912 | tf_op jit(solution)/shard_map/attention_backward/pallas_call | solution.py:529
  403.9 16.7 %collective-permute-done.71 = bf16[4,96,640]{2,1,0:T(8,128)(2,1)S(1)} collective-permute-done((bf16[4,96,640]{2,1,0:T(8,128)(2,1)}, bf16[4,96,640]{2,1,0:T(8,128)(2,1)S(1)}, u32[]{:S(2)}, u32[]{:S(2)}) %collective-permute-start.71) | collective-permute-done | bytes 491552 | tf_op jit(solution)/shard_map/ppermute | solution.py:642
  420.6 6.0 %collective-permute-done.79 = bf16[4,48,768]{2,1,0:T(8,128)(2,1)S(1)} collective-permute-done((bf16[4,48,768]{2,1,0:T(8,128)(2,1)S(1)}, bf16[4,48,768]{2,1,0:T(8,128)(2,1)S(1)}, u32[]{:S(2)}, u32[]{:S(2)}) %collective-permute-start.79) | collective-permute-done | bytes 294944 | tf_op jit(solution)/shard_map/ppermute | solution.py:642
  432.3 23.1 %collective-permute-done.64 = bf16[4,192,768]{2,1,0:T(8,128)(2,1)S(1)} collective-permute-done((bf16[4,192,768]{2,1,0:T(8,128)(2,1)S(1)}, bf16[4,192,768]{2,1,0:T(8,128)(2,1)S(1)}, u32[]{:S(2)}, u32[]{:S(2)}) %collective-permute-start.64) | collective-permute-done | bytes 1179680 | tf_op jit(solution)/shard_map/ppermute | solution.py:642
  461.8 7.8 %collective-permute-done.67 = bf16[192,768]{1,0:T(8,128)(2,1)S(1)} collective-permute-done((bf16[192,768]{1,0:T(8,128)(2,1)S(1)}, bf16[192,768]{1,0:T(8,128)(2,1)S(1)}, u32[]{:S(2)}, u32[]{:S(2)}) %collective-permute-start.67) | collective-permute-done | bytes 294944 | tf_op jit(solution)/shard_map/ppermute | solution.py:642
  469.6 11.5 %collective-permute-start.73 = (bf16[96,640]{1,0:T(8,128)(2,1)S(1)}, bf16[96,640]{1,0:T(8,128)(2,1)S(1)}, u32[]{:S(2)}, u32[]{:S(2)}) collective-permute-start(bf16[96,640]{1,0:T(8,128)(2,1)S(1)} %get-tuple-element.247), channel_id=1, source_target_pairs={{0,16},{4,20},{8,24},{12,28},{16,0},{20,4},{24,8},{28,12},{1,17},{... | collective-permute-start | bytes 368648 | tf_op jit(solution)/shard_map/ppermute | solution.py:642
  481.0 8.5 %collective-permute-start.72 = (bf16[96,640]{1,0:T(8,128)(2,1)S(1)}, bf16[96,640]{1,0:T(8,128)(2,1)S(1)}, u32[]{:S(2)}, u32[]{:S(2)}) collective-permute-start(bf16[96,640]{1,0:T(8,128)(2,1)S(1)} %get-tuple-element.245), channel_id=1, source_target_pairs={{0,24},{4,28},{8,0},{12,4},{16,8},{20,12},{24,16},{28,20},{1,25},{... | collective-permute-start | bytes 368648 | tf_op jit(solution)/shard_map/ppermute | solution.py:642
  503.0 4.9 collective-permute-done.69.m2
  510.9 11.2 %collective-permute-done.76.q2 = bf16[96,640]{1,0:T(8,128)(2,1)S(1)} collective-permute-done((bf16[96,640]{1,0:T(8,128)(2,1)S(1)}, bf16[96,640]{1,0:T(8,128)(2,1)S(1)}, u32[]{:S(2)}, u32[]{:S(2)}) %collective-permute-start.76) | collective-permute-done | bytes 122912 | tf_op jit(solution)/shard_map/ppermute | solution.py:642
  (402 shorter events, 164.6 us)
Async XLA Ops:
  18.6 70.0 %collective-permute-start.3 = (bf16[96,640]{1,0:T(8,128)(2,1)}, bf16[96,640]{1,0:T(8,128)(2,1)}, u32[]{:S(2)}, u32[]{:S(2)}) collective-permute-start(bf16[96,640]{1,0:T(8,128)(2,1)} %get-tuple-element.110.refs_0_), channel_id=1, source_target_pairs={{0,24},{4,28},{8,0},{12,4},{16,8},{20,12},{24,16},{28,20},{1,25},{... | collective-permute-start | bytes 368648 | tf_op jit(solution)/shard_map/ppermute | solution.py:642
  22.5 67.7 %collective-permute-start.4 = (bf16[96,640]{1,0:T(8,128)(2,1)S(1)}, bf16[96,640]{1,0:T(8,128)(2,1)S(1)}, u32[]{:S(2)}, u32[]{:S(2)}) collective-permute-start(bf16[96,640]{1,0:T(8,128)(2,1)S(1)} %copy-done.38), channel_id=1, source_target_pairs={{0,16},{4,20},{8,24},{12,28},{16,0},{20,4},{24,8},{28,12},{1,17},{... | collective-permute-start | bytes 368648 | tf_op jit(solution)/shard_map/ppermute | solution.py:642
  23.1 67.7 %collective-permute-start.5 = (bf16[96,640]{1,0:T(8,128)(2,1)S(1)}, bf16[96,640]{1,0:T(8,128)(2,1)S(1)}, u32[]{:S(2)}, u32[]{:S(2)}) collective-permute-start(bf16[96,640]{1,0:T(8,128)(2,1)S(1)} %copy-done.38), channel_id=1, source_target_pairs={{0,8},{4,12},{8,16},{12,20},{16,24},{20,28},{24,0},{28,4},{1,9},{5... | collective-permute-start | bytes 368648 | tf_op jit(solution)/shard_map/ppermute | solution.py:642
  48.7 43.6 %collective-permute-start.6 = (bf16[96,640]{1,0:T(8,128)(2,1)S(1)}, bf16[96,640]{1,0:T(8,128)(2,1)S(1)}, u32[]{:S(2)}, u32[]{:S(2)}) collective-permute-start(bf16[96,640]{1,0:T(8,128)(2,1)S(1)} %copy-done.38), channel_id=1, source_target_pairs={{0,4},{4,0},{8,12},{12,8},{16,20},{20,16},{24,28},{28,24},{1,5},{5... | collective-permute-start | bytes 368648 | tf_op jit(solution)/shard_map/ppermute | solution.py:642
  50.3 56.6 %collective-permute-start.21 = (bf16[256,768]{1,0:T(8,128)(2,1)S(1)}, bf16[256,768]{1,0:T(8,128)(2,1)S(1)}, u32[]{:S(2)}, u32[]{:S(2)}) collective-permute-start(bf16[256,768]{1,0:T(8,128)(2,1)S(1)} %get-tuple-element.236.x0.x_ref.refs_8_), channel_id=1, source_target_pairs={{0,1},{1,0},{2,3},{3,2},{4,5},{5,4},{6,7},{7,6},{8,9},{9,8},{10,11... | collective-permute-start | bytes 1179656 | tf_op jit(solution)/shard_map/ppermute | solution.py:642
  88.7 102.3 %collective-permute-start.36 = (bf16[4,192,768]{2,1,0:T(8,128)(2,1)}, bf16[4,192,768]{2,1,0:T(8,128)(2,1)}, u32[]{:S(2)}, u32[]{:S(2)}) collective-permute-start(bf16[4,192,768]{2,1,0:T(8,128)(2,1)} %place.5.refs_5_), channel_id=1, source_target_pairs={{0,2},{1,3},{2,0},{3,1},{4,6},{5,7},{6,4},{7,5},{8,10},{9,11},{10,... | collective-permute-start | bytes 3538952 | tf_op jit(solution)/shard_map/ppermute | solution.py:642
  106.9 100.2 %collective-permute-start.40 = (bf16[4,192,768]{2,1,0:T(8,128)(2,1)}, bf16[4,192,768]{2,1,0:T(8,128)(2,1)}, u32[]{:S(2)}, u32[]{:S(2)}) collective-permute-start(bf16[4,192,768]{2,1,0:T(8,128)(2,1)} %place.5.refs_5_), channel_id=1, source_target_pairs={{0,4},{4,0},{8,12},{12,8},{16,20},{20,16},{24,28},{28,24},{1,5},{5... | collective-permute-start | bytes 3538952 | tf_op jit(solution)/shard_map/ppermute | solution.py:642
  155.1 49.9 %collective-permute-start.20 = (bf16[8,48,768]{2,1,0:T(8,128)(2,1)}, bf16[8,48,768]{2,1,0:T(8,128)(2,1)S(1)}, u32[]{:S(2)}, u32[]{:S(2)}) collective-permute-start(bf16[8,48,768]{2,1,0:T(8,128)(2,1)} %place.4), channel_id=1, source_target_pairs={{0,1},{1,0},{2,3},{3,2},{4,5},{5,4},{6,7},{7,6},{8,9},{9,8},{10,11... | collective-permute-start | bytes 1769480 | tf_op jit(solution)/shard_map/ppermute | solution.py:642
  156.3 48.8 %collective-permute-start.2 = (bf16[256,768]{1,0:T(8,128)(2,1)}, bf16[256,768]{1,0:T(8,128)(2,1)}, u32[]{:S(2)}, u32[]{:S(2)}) collective-permute-start(bf16[256,768]{1,0:T(8,128)(2,1)} %collective-permute-done.1.x2.refs_10_), channel_id=1, source_target_pairs={{0,1},{1,0},{2,3},{3,2},{4,5},{5,4},{6,7},{7,6},{8,9},{9,8},{10,11... | collective-permute-start | bytes 1179656 | tf_op jit(solution)/shard_map/ppermute | solution.py:642
  156.3 49.3 %collective-permute-start.26 = (bf16[256,768]{1,0:T(8,128)(2,1)}, bf16[256,768]{1,0:T(8,128)(2,1)}, u32[]{:S(2)}, u32[]{:S(2)}) collective-permute-start(bf16[256,768]{1,0:T(8,128)(2,1)} %collective-permute-done.25.x2.refs_10_), channel_id=1, source_target_pairs={{0,1},{1,0},{2,3},{3,2},{4,5},{5,4},{6,7},{7,6},{8,9},{9,8},{10,11... | collective-permute-start | bytes 1179656 | tf_op jit(solution)/shard_map/ppermute | solution.py:642
  190.9 56.2 %collective-permute-start.37 = (bf16[4,192,768]{2,1,0:T(8,128)(2,1)}, bf16[4,192,768]{2,1,0:T(8,128)(2,1)}, u32[]{:S(2)}, u32[]{:S(2)}) collective-permute-start(bf16[4,192,768]{2,1,0:T(8,128)(2,1)} %collective-permute-done.36.refs_5_), channel_id=1, source_target_pairs={{0,4},{4,0},{8,12},{12,8},{16,20},{20,16},{24,28},{28,24},{1,5},{5... | collective-permute-start | bytes 3538952 | tf_op jit(solution)/shard_map/ppermute | solution.py:642
  205.0 54.0 %collective-permute-start.41 = (bf16[4,192,768]{2,1,0:T(8,128)(2,1)S(1)}, bf16[4,192,768]{2,1,0:T(8,128)(2,1)S(1)}, u32[]{:S(2)}, u32[]{:S(2)}) collective-permute-start(bf16[4,192,768]{2,1,0:T(8,128)(2,1)S(1)} %copy-done.10), channel_id=1, source_target_pairs={{0,1},{1,0},{2,3},{3,2},{4,5},{5,4},{6,7},{7,6},{8,9},{9,8},{10,11... | collective-permute-start | bytes 3538952 | tf_op jit(solution)/shard_map/ppermute | solution.py:642
  207.1 51.9 %collective-permute-start.42 = (bf16[4,192,768]{2,1,0:T(8,128)(2,1)}, bf16[4,192,768]{2,1,0:T(8,128)(2,1)}, u32[]{:S(2)}, u32[]{:S(2)}) collective-permute-start(bf16[4,192,768]{2,1,0:T(8,128)(2,1)} %collective-permute-done.40.refs_6_), channel_id=1, source_target_pairs={{0,1},{1,0},{2,3},{3,2},{4,5},{5,4},{6,7},{7,6},{8,9},{9,8},{10,11... | collective-permute-start | bytes 3538952 | tf_op jit(solution)/shard_map/ppermute | solution.py:642
  247.1 36.9 %collective-permute-start.38 = (bf16[4,192,768]{2,1,0:T(8,128)(2,1)}, bf16[4,192,768]{2,1,0:T(8,128)(2,1)}, u32[]{:S(2)}, u32[]{:S(2)}) collective-permute-start(bf16[4,192,768]{2,1,0:T(8,128)(2,1)} %collective-permute-done.36.refs_5_), channel_id=1, source_target_pairs={{0,1},{1,0},{2,3},{3,2},{4,5},{5,4},{6,7},{7,6},{8,9},{9,8},{10,11... | collective-permute-start | bytes 3538952 | tf_op jit(solution)/shard_map/ppermute | solution.py:642
  247.1 36.9 %collective-permute-start.39 = (bf16[4,192,768]{2,1,0:T(8,128)(2,1)}, bf16[4,192,768]{2,1,0:T(8,128)(2,1)}, u32[]{:S(2)}, u32[]{:S(2)}) collective-permute-start(bf16[4,192,768]{2,1,0:T(8,128)(2,1)} %collective-permute-done.37.refs_6_), channel_id=1, source_target_pairs={{0,1},{1,0},{2,3},{3,2},{4,5},{5,4},{6,7},{7,6},{8,9},{9,8},{10,11... | collective-permute-start | bytes 3538952 | tf_op jit(solution)/shard_map/ppermute | solution.py:642
  283.1 40.9 %collective-permute-start.59 = (bf16[4,192,768]{2,1,0:T(8,128)(2,1)}, bf16[4,192,768]{2,1,0:T(8,128)(2,1)S(1)}, u32[]{:S(2)}, u32[]{:S(2)}) collective-permute-start(bf16[4,192,768]{2,1,0:T(8,128)(2,1)} %get-tuple-element.187), channel_id=1, source_target_pairs={{0,1},{1,0},{2,3},{3,2},{4,5},{5,4},{6,7},{7,6},{8,9},{9,8},{10,11... | collective-permute-start | bytes 3538952 | tf_op jit(solution)/shard_map/ppermute | solution.py:642
  312.7 61.7 %collective-permute-start.53 = (bf16[192,256]{1,0:T(8,128)(2,1)}, bf16[192,256]{1,0:T(8,128)(2,1)S(1)}, u32[]{:S(2)}, u32[]{:S(2)}) collective-permute-start(bf16[192,256]{1,0:T(8,128)(2,1)} %get-tuple-element.169), channel_id=1, source_target_pairs={{0,1},{1,0},{2,3},{3,2},{4,5},{5,4},{6,7},{7,6},{8,9},{9,8},{10,11... | collective-permute-start | bytes 294920 | tf_op jit(solution)/shard_map/ppermute | solution.py:642
  332.1 42.8 %collective-permute-start.54 = (bf16[192,256]{1,0:T(8,128)(2,1)S(1)}, bf16[192,256]{1,0:T(8,128)(2,1)S(1)}, u32[]{:S(2)}, u32[]{:S(2)}) collective-permute-start(bf16[192,256]{1,0:T(8,128)(2,1)S(1)} %copy-done.84), channel_id=1, source_target_pairs={{0,2},{1,3},{2,0},{3,1},{4,6},{5,7},{6,4},{7,5},{8,10},{9,11},{10,... | collective-permute-start | bytes 294920 | tf_op jit(solution)/shard_map/ppermute | solution.py:642
  354.5 46.1 %collective-permute-start.61 = (bf16[4,192,768]{2,1,0:T(8,128)(2,1)}, bf16[4,192,768]{2,1,0:T(8,128)(2,1)}, u32[]{:S(2)}, u32[]{:S(2)}) collective-permute-start(bf16[4,192,768]{2,1,0:T(8,128)(2,1)} %get-tuple-element.189), channel_id=1, source_target_pairs={{0,1},{1,0},{2,3},{3,2},{4,5},{5,4},{6,7},{7,6},{8,9},{9,8},{10,11... | collective-permute-start | bytes 3538952 | tf_op jit(solution)/shard_map/ppermute | solution.py:642
  355.9 44.8 %collective-permute-start.63 = (bf16[4,192,768]{2,1,0:T(8,128)(2,1)S(1)}, bf16[4,192,768]{2,1,0:T(8,128)(2,1)}, u32[]{:S(2)}, u32[]{:S(2)}) collective-permute-start(bf16[4,192,768]{2,1,0:T(8,128)(2,1)S(1)} %add_convert_fusion.2), channel_id=1, source_target_pairs={{0,4},{4,0},{8,12},{12,8},{16,20},{20,16},{24,28},{28,24},{1,5},{5... | collective-permute-start | bytes 3538952 | tf_op jit(solution)/shard_map/ppermute | solution.py:642
  374.4 56.0 %collective-permute-start.58 = (bf16[4,192,768]{2,1,0:T(8,128)(2,1)}, bf16[4,192,768]{2,1,0:T(8,128)(2,1)}, u32[]{:S(2)}, u32[]{:S(2)}) collective-permute-start(bf16[4,192,768]{2,1,0:T(8,128)(2,1)} %get-tuple-element.185), channel_id=1, source_target_pairs={{0,1},{1,0},{2,3},{3,2},{4,5},{5,4},{6,7},{7,6},{8,9},{9,8},{10,11... | collective-permute-start | bytes 3538952 | tf_op jit(solution)/shard_map/ppermute | solution.py:642
  374.8 57.5 %collective-permute-start.60 = (bf16[4,192,768]{2,1,0:T(8,128)(2,1)S(1)}, bf16[4,192,768]{2,1,0:T(8,128)(2,1)}, u32[]{:S(2)}, u32[]{:S(2)}) collective-permute-start(bf16[4,192,768]{2,1,0:T(8,128)(2,1)S(1)} %add_convert_fusion.5), channel_id=1, source_target_pairs={{0,4},{4,0},{8,12},{12,8},{16,20},{20,16},{24,28},{28,24},{1,5},{5... | collective-permute-start | bytes 3538952 | tf_op jit(solution)/shard_map/ppermute | solution.py:642
  428.2 64.0 %collective-permute-start.46 = (bf16[512,768]{1,0:T(8,128)(2,1)S(1)}, bf16[512,768]{1,0:T(8,128)(2,1)S(1)}, u32[]{:S(2)}, u32[]{:S(2)}) collective-permute-start(bf16[512,768]{1,0:T(8,128)(2,1)S(1)} %copy-done.73), channel_id=1, source_target_pairs={{0,1},{1,0},{2,3},{3,2},{4,5},{5,4},{6,7},{7,6},{8,9},{9,8},{10,11... | collective-permute-start | bytes 2359304 | tf_op jit(solution)/shard_map/ppermute | solution.py:642
  429.3 60.7 %collective-permute-start.74 = (bf16[96,640]{1,0:T(8,128)(2,1)S(1)}, bf16[96,640]{1,0:T(8,128)(2,1)S(1)}, u32[]{:S(2)}, u32[]{:S(2)}) collective-permute-start(bf16[96,640]{1,0:T(8,128)(2,1)S(1)} %get-tuple-element.246), channel_id=1, source_target_pairs={{0,8},{4,12},{8,16},{12,20},{16,24},{20,28},{24,0},{28,4},{1,9},{5... | collective-permute-start | bytes 368648 | tf_op jit(solution)/shard_map/ppermute | solution.py:642
  (152 other events, 2758.8 us)
